TPU v7x, 32 devices: a whole 2x2x4 slice. The times are simulated.
32 devices in a mesh: dp: 4 (over y, x), fsdp: 8 (over z, core).
Axes of the slice: x: 2, y: 2, z: 4, core: 2. Of those that a mesh axis runs over, the one named last changes fastest.
Arguments:
- latents: bfloat16 [32, 128, 16, 8], P(('dp', 'fsdp')), may hold values from -6 to 6
- noises: bfloat16 [32, 128, 16, 8], P(('dp', 'fsdp')), may hold values from -6 to 6
- clap_embed: float32 [32, 512], P(('dp', 'fsdp')), may hold values from -6 to 6
- timesteps: int32 [32], P(('dp', 'fsdp')), may hold values from 0 to 999
- lengths: int32 [32], P(('dp', 'fsdp')), may hold values from 32 to 128, as said below
- step_count: int32 [1], replicated, may hold values from 2 to 20
- stem_w: float32 [72, 256], replicated, may hold values from -0.75 to 0.75
- head_w: float32 [2304, 8], replicated, may hold values from -0.125 to 0.125
- time_w: float32 [3, 512, 512], P(None, 'fsdp'), may hold values from -0.25 to 0.25
- vector: float32 [5896], replicated
- conv_w: float32 [2, 2304, 256], P(None, 'fsdp'), may hold values from -0.125 to 0.125
- wide_w: float32 [256, 2048], P('fsdp'), may hold values from -0.375 to 0.375
- down_w: float32 [1024, 256], P('fsdp'), may hold values from -0.1875 to 0.1875
- roots_small: float32 [5, 256, 256], replicated, as said below
- root_wide: float32 [768, 768], replicated, as said below
- roots_large: float32 [2, 1024, 1024], replicated, as said below
- stem_moment: float32 [72, 256], replicated
- stem_square: float32 [72, 256], replicated, as said below
- head_moment: float32 [2304, 8], replicated
- head_square: float32 [2304, 8], replicated, as said below
- time_moment: float32 [3, 512, 512], P(None, 'fsdp')
- time_square: float32 [3, 512, 512], P(None, 'fsdp'), as said below
- vector_moment: float32 [5896], replicated
- vector_square: float32 [5896], replicated, as said below
- conv_moment: float32 [2, 2304, 256], P(None, 'fsdp')
- conv_square: float32 [2, 2304, 256], P(None, 'fsdp'), as said below
- wide_moment: float32 [256, 2048], P('fsdp')
- down_moment: float32 [1024, 256], P('fsdp')
Outputs:
- loss_value: float32 [], replicated
- grad_norm: float32 [], replicated
- stem_new: float32 [72, 256], replicated
- stem_moment_new: float32 [72, 256], replicated
- stem_square_new: float32 [72, 256], replicated
- head_new: float32 [2304, 8], replicated
- head_moment_new: float32 [2304, 8], replicated
- head_square_new: float32 [2304, 8], replicated
- time_new: float32 [3, 512, 512], P(None, 'fsdp')
- time_moment_new: float32 [3, 512, 512], P(None, 'fsdp')
- time_square_new: float32 [3, 512, 512], P(None, 'fsdp')
- vector_grad: float32 [5896], replicated
- vector_moment_new: float32 [5896], replicated
- vector_square_new: float32 [5896], replicated
- conv_new: float32 [2, 2304, 256], P(None, 'fsdp')
- conv_moment_new: float32 [2, 2304, 256], P(None, 'fsdp')
- conv_square_new: float32 [2, 2304, 256], P(None, 'fsdp')
- wide_new: float32 [256, 2048], P('fsdp')
- wide_moment_new: float32 [256, 2048], P('fsdp')
- down_new: float32 [1024, 256], P('fsdp')
- down_moment_new: float32 [1024, 256], P('fsdp')
Inputs may be any that keep to these rules, and one draw needn't show every extreme that they name: `lengths`: each clip's live latent frames; clip 0 has 128. `roots_small`: symmetric and positive definite. `root_wide`: symmetric and positive definite. `roots_large`: symmetric and positive definite. `stem_square`: positive. `head_square`: positive. `time_square`: positive. `vector_square`: positive. `conv_square`: positive.
All inputs are finite; a program needn't handle non-finite values.
Results may differ from a plain program's by a relative error of at most 0.013.
Values may be sent and summed in bfloat16 or wider, within the bound.
A program may use at most 320 MiB of HBM per device.

v0:
```python
import math

import jax
import jax.numpy as jnp
from jax import lax
from jax.sharding import PartitionSpec as P

HEADS = 8
FF = 1024
EMB = 512
GROUPS = 32


highest = lax.Precision.HIGHEST
norm_floor = 1e-05
masked_score = -1e30
clip_limit = 0.002
adam_rate = 0.05
adam_floor = 1e-08
shampoo_rate = 0.02
decay_rate = 0.01


def split_up(value, dim, count):
    dims = value.shape
    pieces = value.reshape(*dims[:dim], count, dims[dim] // count, *dims[dim + 1 :])
    return jnp.moveaxis(pieces, dim, 0)


def sum_at_owner(value, axis, dim):
    count = lax.axis_size(axis)
    pieces = lax.all_to_all(split_up(value, dim, count), axis, 0, 0, tiled=True)
    return jnp.sum(pieces.astype(jnp.float32), axis=0)


def matmul(left_op, right_op):
    return jnp.dot(left_op, right_op, preferred_element_type=jnp.float32)


def inner_rows(left_op, right_op):
    return lax.dot_general(
        left_op, right_op, (((0,), (0,)), ((), ())), preferred_element_type=jnp.float32
    )


def outer_cols(left_op, right_op):
    return lax.dot_general(
        left_op, right_op, (((1,), (1,)), ((), ())), preferred_element_type=jnp.float32
    )


def patches(flat, frames_n, freq_bins):
    channels = flat.shape[-1]
    padded = jnp.pad(flat.reshape(frames_n, freq_bins, channels), ((1, 1), (1, 1), (0, 0)))
    shifted = [padded[a : a + frames_n, b : b + freq_bins] for a in range(3) for b in range(3)]
    return jnp.stack(shifted, 2).reshape(frames_n * freq_bins, 9 * channels)


def unpatch(columns, frames_n, freq_bins):
    channels = columns.shape[-1] // 9
    tap_split = columns.reshape(frames_n, freq_bins, 9, channels)
    padded = jnp.zeros((frames_n + 2, freq_bins + 2, channels), jnp.float32)
    for a in range(3):
        for b in range(3):
            padded = padded + jnp.pad(tap_split[:, :, 3 * a + b], ((a, 2 - a), (b, 2 - b), (0, 0)))
    return padded[1:-1, 1:-1].reshape(frames_n * freq_bins, channels)


def split_vector(vector, channels, embed_width, hidden_units, latent_ch):
    lengths_list = [channels] * 13 + [embed_width] * 3 + [hidden_units, latent_ch]
    pieces = []
    offset = 0
    for seg_len in lengths_list:
        pieces.append(vector[offset : offset + seg_len])
        offset = offset + seg_len
    return pieces


def group_norm(field, gain, shift, pix_mask, groups):
    frames_n, freq_bins, channels = field.shape
    grouped = field.reshape(frames_n, freq_bins, groups, channels // groups)
    mask_grid = pix_mask.reshape(frames_n, freq_bins, 1, 1)
    counted = jnp.sum(mask_grid) * (channels // groups)
    center = jnp.sum(grouped * mask_grid, axis=(0, 1, 3), keepdims=True) / counted
    spread = jnp.sum(mask_grid * (grouped - center) ** 2, axis=(0, 1, 3), keepdims=True) / counted
    normed = ((grouped - center) * lax.rsqrt(spread + norm_floor)).reshape(field.shape)
    return normed * gain + shift


def layer_norm(row_field, gain, shift):
    center = jnp.mean(row_field, axis=-1, keepdims=True)
    spread = jnp.mean((row_field - center) ** 2, axis=-1, keepdims=True)
    return (row_field - center) * lax.rsqrt(spread + norm_floor) * gain + shift


def noise_mix(step_value):
    phase = (step_value.astype(jnp.float32) / 1000.0 + 0.008) / 1.008 * (math.pi / 2)
    keep_part = jnp.cos(phase) ** 2
    return (jnp.sqrt(keep_part), jnp.sqrt(1.0 - keep_part))


def film_terms(time_w, bias_one, bias_two, bias_film, step_value, clap_row):
    half_width = time_w.shape[1] // 2
    frequency = jnp.exp(
        -math.log(10000.0) * jnp.arange(half_width).astype(jnp.float32) / half_width
    )
    angles = step_value.astype(jnp.float32) * frequency
    sinusoid = jnp.concatenate([jnp.cos(angles), jnp.sin(angles)])
    hidden = jax.nn.silu(jnp.dot(sinusoid, time_w[0], precision=highest) + bias_one)
    embedding = jnp.dot(hidden, time_w[1], precision=highest) + bias_two + clap_row
    return jnp.dot(jax.nn.silu(embedding), time_w[2], precision=highest) + bias_film


def head_split(proj_qkv, head_count):
    rows_n, triple = proj_qkv.shape
    channels = triple // 3
    head_dim = channels // head_count
    block_rows = min(512, rows_n)
    queries = proj_qkv[:, :channels].reshape(rows_n // block_rows, block_rows, head_count, head_dim)
    key_heads = proj_qkv[:, channels : 2 * channels].reshape(rows_n, head_count, head_dim)
    value_heads = proj_qkv[:, 2 * channels :].reshape(rows_n, head_count, head_dim)
    return (queries, key_heads, value_heads, head_dim ** (-0.5))


def block_scores(query_block, key_heads, key_live, factor):
    scores = (
        jnp.einsum("qhd,khd->hqk", query_block, key_heads, preferred_element_type=jnp.float32)
        * factor
    )
    return jnp.where(key_live[None, None, :], scores, masked_score)


def attend(proj_qkv, key_live, head_count):
    queries, key_heads, value_heads, factor = head_split(proj_qkv, head_count)

    def one_block(query_block):
        scores = block_scores(query_block, key_heads, key_live, factor)
        row_top = jnp.max(scores, axis=-1, keepdims=True)
        lifted = jnp.exp(scores - row_top)
        denominator = jnp.sum(lifted, axis=-1, keepdims=True)
        soft_weights = (lifted / denominator).astype(jnp.bfloat16)
        mixed_block = jnp.einsum(
            "hqk,khd->qhd", soft_weights, value_heads, preferred_element_type=jnp.float32
        )
        flat_block = mixed_block.astype(jnp.bfloat16).reshape(query_block.shape[0], -1)
        return (flat_block, (row_top + jnp.log(denominator))[:, :, 0])

    mixed_out, log_total = lax.map(one_block, queries)
    return (mixed_out.reshape(proj_qkv.shape[0], -1), log_total)


def attend_back(proj_qkv, log_total, grad_mixed, key_live, head_count):
    queries, key_heads, value_heads, factor = head_split(proj_qkv, head_count)
    grad_blocks = grad_mixed.reshape(queries.shape)

    def one_block(running, block_item):
        grad_keys, grad_values = running
        query_block, total_block, grad_block = block_item
        scores = block_scores(query_block, key_heads, key_live, factor)
        soft_weights = jnp.exp(scores - total_block[:, :, None])
        grad_soft = jnp.einsum(
            "qhd,khd->hqk", grad_block, value_heads, preferred_element_type=jnp.float32
        )
        weighted = jnp.sum(soft_weights * grad_soft, axis=-1, keepdims=True)
        grad_raw = (factor * soft_weights * (grad_soft - weighted)).astype(jnp.bfloat16)
        grad_query = jnp.einsum(
            "hqk,khd->qhd", grad_raw, key_heads, preferred_element_type=jnp.float32
        )
        grad_keys = grad_keys + jnp.einsum(
            "hqk,qhd->khd", grad_raw, query_block, preferred_element_type=jnp.float32
        )
        grad_values = grad_values + jnp.einsum(
            "hqk,qhd->khd",
            soft_weights.astype(jnp.bfloat16),
            grad_block,
            preferred_element_type=jnp.float32,
        )
        return ((grad_keys, grad_values), grad_query)

    zeros_kv = jnp.zeros(key_heads.shape, jnp.float32)
    (grad_keys, grad_values), grad_query = lax.scan(
        one_block, (zeros_kv, zeros_kv), (queries, log_total, grad_blocks)
    )
    rows_n = proj_qkv.shape[0]
    joined = jnp.concatenate(
        [
            grad_query.reshape(rows_n, -1),
            grad_keys.reshape(rows_n, -1),
            grad_values.reshape(rows_n, -1),
        ],
        1,
    )
    return joined.astype(jnp.bfloat16)


def adam_step(weight, moment_one, moment_two, gradient, decay_on, fix_one, fix_two):
    first_new = 0.9 * moment_one + 0.1 * gradient
    second_new = 0.999 * moment_two + 0.001 * gradient * gradient
    moved = first_new / fix_one / (jnp.sqrt(second_new / fix_two) + adam_floor)
    return (weight - adam_rate * (moved + decay_on * weight), first_new, second_new)


def precondition(moment, left_root, right_root):
    rows_here = moment.shape[0]
    right_done = jnp.dot(moment, right_root, precision=highest)
    left_cols = lax.dynamic_slice_in_dim(
        left_root, lax.axis_index("fsdp") * rows_here, rows_here, 1
    )
    return sum_at_owner(
        jnp.dot(left_cols, right_done, precision=highest).astype(jnp.bfloat16), "fsdp", 0
    )


def local(
    latents,
    noises,
    clap_embed,
    timesteps,
    lengths,
    step_count,
    stem_w,
    head_w,
    time_w,
    vector,
    conv_w,
    wide_w,
    down_w,
    roots_small,
    root_wide,
    roots_large,
    stem_moment,
    stem_square,
    head_moment,
    head_square,
    time_moment,
    time_square,
    vector_moment,
    vector_square,
    conv_moment,
    conv_square,
    wide_moment,
    down_moment,
):
    frames_n, freq_bins, latent_ch = (latents.shape[1], latents.shape[2], latents.shape[3])
    channels = stem_w.shape[1]
    rows_n = frames_n * freq_bins
    segs = split_vector(vector, channels, EMB, FF, latent_ch)
    key_live = jnp.repeat(jnp.arange(frames_n) < lengths[0], freq_bins)
    pix_mask = key_live.astype(jnp.float32)[:, None]
    live_count = lax.psum(jnp.sum(pix_mask), ("dp", "fsdp"))
    time_full = lax.all_gather(time_w, "fsdp", axis=1, tiled=True)
    conv_full, wide_full, down_full = (
        lax.all_gather(conv_w.astype(jnp.bfloat16), "fsdp", axis=1, tiled=True),
        lax.all_gather(wide_w.astype(jnp.bfloat16), "fsdp", axis=0, tiled=True),
        lax.all_gather(down_w.astype(jnp.bfloat16), "fsdp", axis=0, tiled=True),
    )

    def first_act(stream_in, gain, shift):
        normed = group_norm(
            stream_in.reshape(frames_n, freq_bins, channels), gain, shift, pix_mask, GROUPS
        )
        return jax.nn.silu(normed).reshape(rows_n, channels) * pix_mask

    def second_act(inner_in, film_in, gain, shift):
        moved = inner_in * (1.0 + film_in[:channels]) + film_in[channels:]
        normed = group_norm(
            moved.reshape(frames_n, freq_bins, channels), gain, shift, pix_mask, GROUPS
        )
        return jax.nn.silu(normed).reshape(rows_n, channels) * pix_mask

    def film_local(time_in, bias_one, bias_two, bias_film):
        return film_terms(time_in, bias_one, bias_two, bias_film, timesteps[0], clap_embed[0])

    def gelu_exact(values_in):
        return jax.nn.gelu(values_in, approximate=False)

    keep_root, noise_root = noise_mix(timesteps[0])
    noise_rows = noises[0].astype(jnp.float32).reshape(rows_n, latent_ch)
    clean_rows = latents[0].astype(jnp.float32).reshape(rows_n, latent_ch)
    noisy = ((keep_root * clean_rows + noise_root * noise_rows) * pix_mask).astype(jnp.bfloat16)
    noisy_cols = patches(noisy, frames_n, freq_bins)
    stream_zero = matmul(noisy_cols, stem_w.astype(jnp.bfloat16)) + segs[12]
    act_one = first_act(stream_zero, segs[0], segs[1]).astype(jnp.bfloat16)
    inner_out = matmul(patches(act_one, frames_n, freq_bins), conv_full[0]) + segs[2]
    film_out = film_local(time_full, segs[13], segs[14], segs[15])
    act_two = second_act(inner_out, film_out, segs[3], segs[4]).astype(jnp.bfloat16)
    stream_one = stream_zero + matmul(patches(act_two, frames_n, freq_bins), conv_full[1]) + segs[5]
    normed_one = layer_norm(stream_one, segs[6], segs[7]).astype(jnp.bfloat16)
    proj_qkv = matmul(normed_one, wide_full[:, : 3 * channels]).astype(jnp.bfloat16)
    mixed_out, log_total = attend(proj_qkv, key_live, HEADS)
    stream_two = stream_one + matmul(mixed_out, wide_full[:, 3 * channels : 4 * channels]) + segs[8]
    normed_two = layer_norm(stream_two, segs[9], segs[10]).astype(jnp.bfloat16)
    pre_act = matmul(normed_two, wide_full[:, 4 * channels :]) + segs[16]
    hidden = gelu_exact(pre_act).astype(jnp.bfloat16)
    stream_three = stream_two + matmul(hidden, down_full) + segs[11]
    head_cols = patches((stream_three * pix_mask).astype(jnp.bfloat16), frames_n, freq_bins)
    head_low = head_w.astype(jnp.bfloat16)
    predicted = matmul(head_cols, head_low) + segs[17]
    errors = (predicted - noise_rows) * pix_mask
    loss_local = jnp.sum(errors * errors)
    conv_back, wide_back, down_back = (
        lax.all_gather(conv_w.astype(jnp.bfloat16), "fsdp", axis=1, tiled=True),
        lax.all_gather(wide_w.astype(jnp.bfloat16), "fsdp", axis=0, tiled=True),
        lax.all_gather(down_w.astype(jnp.bfloat16), "fsdp", axis=0, tiled=True),
    )
    grad_pred = 2.0 * errors / (latent_ch * live_count)
    grad_head_b = jnp.sum(grad_pred, 0)
    grad_pred_low = grad_pred.astype(jnp.bfloat16)
    grad_head_w = inner_rows(head_cols, grad_pred_low)
    grad_three = unpatch(outer_cols(grad_pred_low, head_low), frames_n, freq_bins) * pix_mask
    grad_down_b = jnp.sum(grad_three, 0)
    grad_three_low = grad_three.astype(jnp.bfloat16)
    grad_down_w = inner_rows(hidden, grad_three_low)
    grad_hidden = outer_cols(grad_three_low, down_back)
    _, gelu_back = jax.vjp(gelu_exact, pre_act)
    grad_pre = gelu_back(grad_hidden)[0]
    grad_up_b = jnp.sum(grad_pre, 0)
    grad_pre_low = grad_pre.astype(jnp.bfloat16)
    grad_up_w = inner_rows(normed_two, grad_pre_low)
    _, norm_two_back = jax.vjp(layer_norm, stream_two, segs[9], segs[10])
    back_two, grad_ln2_g, grad_ln2_b = norm_two_back(
        outer_cols(grad_pre_low, wide_back[:, 4 * channels :])
    )
    grad_two = grad_three + back_two
    grad_proj_b = jnp.sum(grad_two, 0)
    grad_two_low = grad_two.astype(jnp.bfloat16)
    grad_proj_w = inner_rows(mixed_out, grad_two_low)
    grad_mixed = outer_cols(grad_two_low, wide_back[:, 3 * channels : 4 * channels]).astype(
        jnp.bfloat16
    )
    grad_qkv = attend_back(proj_qkv, log_total, grad_mixed, key_live, HEADS)
    grad_qkv_w = inner_rows(normed_one, grad_qkv)
    _, norm_one_back = jax.vjp(layer_norm, stream_one, segs[6], segs[7])
    back_one, grad_ln1_g, grad_ln1_b = norm_one_back(
        outer_cols(grad_qkv, wide_back[:, : 3 * channels])
    )
    grad_one = grad_two + back_one
    grad_conv2_b = jnp.sum(grad_one, 0)
    grad_one_low = grad_one.astype(jnp.bfloat16)
    grad_conv_two = inner_rows(patches(act_two, frames_n, freq_bins), grad_one_low)
    grad_act_two = unpatch(outer_cols(grad_one_low, conv_back[1]), frames_n, freq_bins)
    _, second_back = jax.vjp(second_act, inner_out, film_out, segs[3], segs[4])
    grad_inner, grad_film, grad_gn2_g, grad_gn2_b = second_back(grad_act_two)
    grad_conv1_b = jnp.sum(grad_inner, 0)
    grad_inner_low = grad_inner.astype(jnp.bfloat16)
    grad_conv_one = inner_rows(patches(act_one, frames_n, freq_bins), grad_inner_low)
    grad_act_one = unpatch(outer_cols(grad_inner_low, conv_back[0]), frames_n, freq_bins)
    _, first_back = jax.vjp(first_act, stream_zero, segs[0], segs[1])
    back_zero, grad_gn1_g, grad_gn1_b = first_back(grad_act_one)
    grad_zero = grad_one + back_zero
    grad_stem_b = jnp.sum(grad_zero, 0)
    grad_stem_w = inner_rows(noisy_cols, grad_zero.astype(jnp.bfloat16))
    _, film_back = jax.vjp(film_local, time_full, segs[13], segs[14], segs[15])
    grad_time_w, grad_tb_one, grad_tb_two, grad_film_b = film_back(grad_film)
    grad_vector = jnp.concatenate(
        [
            grad_gn1_g,
            grad_gn1_b,
            grad_conv1_b,
            grad_gn2_g,
            grad_gn2_b,
            grad_conv2_b,
            grad_ln1_g,
            grad_ln1_b,
            grad_proj_b,
            grad_ln2_g,
            grad_ln2_b,
            grad_down_b,
            grad_stem_b,
            grad_tb_one,
            grad_tb_two,
            grad_film_b,
            grad_up_b,
            grad_head_b,
        ]
    )
    grad_conv = jnp.stack([grad_conv_one, grad_conv_two])
    grad_wide = jnp.concatenate([grad_qkv_w, grad_proj_w, grad_up_w], 1)
    time_shard, conv_shard, wide_shard, down_shard = (
        lax.psum_scatter(grad_time_w, "fsdp", scatter_dimension=1, tiled=True),
        lax.psum_scatter(grad_conv, "fsdp", scatter_dimension=1, tiled=True),
        lax.psum_scatter(grad_wide, "fsdp", scatter_dimension=0, tiled=True),
        lax.psum_scatter(grad_down_w, "fsdp", scatter_dimension=0, tiled=True),
    )
    time_shard, conv_shard, wide_shard, down_shard = (
        lax.psum(time_shard.astype(jnp.bfloat16), "dp").astype(jnp.float32),
        lax.psum(conv_shard.astype(jnp.bfloat16), "dp").astype(jnp.float32),
        lax.psum(wide_shard.astype(jnp.bfloat16), "dp").astype(jnp.float32),
        lax.psum(down_shard.astype(jnp.bfloat16), "dp").astype(jnp.float32),
    )
    shard_squares = (
        jnp.sum(time_shard * time_shard)
        + jnp.sum(conv_shard * conv_shard)
        + jnp.sum(wide_shard * wide_shard)
        + jnp.sum(down_shard * down_shard)
    )
    loss_sum, grad_stem, grad_head, grad_vec = lax.psum(
        (loss_local, grad_stem_w, grad_head_w, grad_vector), ("dp", "fsdp")
    )
    shard_total = lax.psum(shard_squares, "fsdp")
    loss_value = loss_sum / (latent_ch * live_count)
    replicated_squares = (
        jnp.sum(grad_stem * grad_stem)
        + jnp.sum(grad_head * grad_head)
        + jnp.sum(grad_vec * grad_vec)
    )
    grad_norm = jnp.sqrt(shard_total + replicated_squares)
    factor = jnp.minimum(1.0, clip_limit / grad_norm)
    step_value = step_count[0].astype(jnp.float32)
    fix_one = 1.0 - jnp.power(0.9, step_value)
    fix_two = 1.0 - jnp.power(0.999, step_value)
    vector_clipped = factor * grad_vec
    stem_out = adam_step(
        stem_w, stem_moment, stem_square, factor * grad_stem, decay_rate, fix_one, fix_two
    )
    head_out = adam_step(
        head_w, head_moment, head_square, factor * grad_head, decay_rate, fix_one, fix_two
    )
    time_out = adam_step(
        time_w, time_moment, time_square, factor * time_shard, decay_rate, fix_one, fix_two
    )
    vector_out = adam_step(
        vector, vector_moment, vector_square, vector_clipped, 0.0, fix_one, fix_two
    )
    conv_out = adam_step(
        conv_w, conv_moment, conv_square, factor * conv_shard, decay_rate, fix_one, fix_two
    )
    wide_moment_new = 0.9 * wide_moment + factor * wide_shard
    down_moment_new = 0.9 * down_moment + factor * down_shard
    bounds = (0, 3 * channels, 4 * channels, 4 * channels + FF)
    lefts = (roots_small[0], roots_small[1], roots_small[2])
    rights = (root_wide, roots_small[3], roots_large[0])
    directions = []
    for index_block in range(3):
        directions.append(
            precondition(
                wide_moment_new[:, bounds[index_block] : bounds[index_block + 1]],
                lefts[index_block],
                rights[index_block],
            )
        )
    wide_new = wide_w * (1.0 - shampoo_rate * decay_rate) - shampoo_rate * jnp.concatenate(
        directions, 1
    )
    down_direction = precondition(down_moment_new, roots_large[1], roots_small[4])
    down_new = down_w * (1.0 - shampoo_rate * decay_rate) - shampoo_rate * down_direction
    return (
        loss_value,
        grad_norm,
        stem_out[0],
        stem_out[1],
        stem_out[2],
        head_out[0],
        head_out[1],
        head_out[2],
        time_out[0],
        time_out[1],
        time_out[2],
        vector_clipped,
        vector_out[1],
        vector_out[2],
        conv_out[0],
        conv_out[1],
        conv_out[2],
        wide_new,
        wide_moment_new,
        down_new,
        down_moment_new,
    )


def solution(mesh):
    in_specs = (
        P(("dp", "fsdp"), None, None, None),
        P(("dp", "fsdp"), None, None, None),
        P(("dp", "fsdp"), None),
        P(("dp", "fsdp")),
        P(("dp", "fsdp")),
        P(),
        P(),
        P(),
        P(None, "fsdp", None),
        P(),
        P(None, "fsdp", None),
        P("fsdp", None),
        P("fsdp", None),
        P(),
        P(),
        P(),
        P(),
        P(),
        P(),
        P(),
        P(None, "fsdp", None),
        P(None, "fsdp", None),
        P(),
        P(),
        P(None, "fsdp", None),
        P(None, "fsdp", None),
        P("fsdp", None),
        P("fsdp", None),
    )
    out_specs = (
        P(),
        P(),
        P(),
        P(),
        P(),
        P(),
        P(),
        P(),
        P(None, "fsdp", None),
        P(None, "fsdp", None),
        P(None, "fsdp", None),
        P(),
        P(),
        P(),
        P(None, "fsdp", None),
        P(None, "fsdp", None),
        P(None, "fsdp", None),
        P("fsdp", None),
        P("fsdp", None),
        P("fsdp", None),
        P("fsdp", None),
    )
    return jax.shard_map(local, mesh=mesh, in_specs=in_specs, out_specs=out_specs, check_vma=False)
```

profile of v0, /device:TPU:0, one launch (start us, length us, event | category | flops | bytes accessed | tf_op | source)
XLA Modules:
  0.0 1483.2 jit_solution(8930705979389119383)
XLA Ops:
  15.9 43.1 %psum.71 = f32[]{:T(128)} all-reduce(f32[]{:T(128)} %broadcast_reduce_fusion), channel_id=1, replica_groups=mesh['dp'=4,'fsdp'=8] {'dp','fsdp'}, use_global_device_ids=true, to_apply=%region_19.20 | all-reduce | flops 1 | bytes 8 | tf_op jit(solution)/shard_map/psum | solution.py:250
  61.3 17.9 %all_gather.18 = bf16[1024,256]{1,0:T(8,128)(2,1)} all-gather(bf16[128,256]{1,0:T(8,128)(2,1)S(1)} %convert_element_type.267), channel_id=1, replica_groups=mesh['dp'=4,'fsdp'=8] {'fsdp'}, dimensions={0}, use_global_device_ids=true | all-gather | bytes 589824 | tf_op jit(solution)/shard_map/all_gather | solution.py:255
  97.4 10.7 copy.154
  142.5 10.7 copy.155
  153.3 11.6 copy.228
  181.4 193.5 %while.28 = (s32[]{:T(128)}, bf16[4,512,256]{2,1,0:T(8,128)(2,1)}, f32[4,8,512]{2,1,0:T(8,128)}, bf16[4,512,8,32]{1,3,2,0:T(8,128)(2,1)}, bf16[2048,8,32]{0,2,1:...) while((s32[]{:T(128)}, bf16[4,512,256]{2,1,0:T(8,128)(2,1)}, ...), condition=%wide.region_14.15_spmd.clone, body=%wide.region_11.14_spmd.clone.sunk | while | flops 1174532096 | bytes 104476904 | solution.py:148
  181.8 14.2 fusion.302
  196.0 14.5 fusion.303
  210.5 15.4 %fusion.304 = bf16[8,512,32]{1,2,0:T(8,128)(2,1)} fusion(bf16[2048,8,32]{0,2,1:T(8,128)(2,1)} %get-tuple-element.526, f32[8,512,2048]{2,1,0:T(8,128)} %get-tuple-element.491, f32[8,512]{1,0:T(8,128)S(1)} %fusion.303, f32[8,512]{1,0:T(8,128)S(1)} %get-tuple-element.492, pred[2048]{0:T(1024)(128)(4,1)S(1)} %broadcast_in_dim.230), kind=kOutput, calls=%fused_computation.8.clone.1 | convolution fusion | flops 578945024 | bytes 34899968 | tf_op jit(solution)/shard_map/while/body/eval_jaxpr/hqk,khd->qhd/dot_general | solution.py:142
  230.1 14.2 fusion.302
  244.3 14.5 fusion.303
  258.8 15.4 %fusion.304 = bf16[8,512,32]{1,2,0:T(8,128)(2,1)} fusion(bf16[2048,8,32]{0,2,1:T(8,128)(2,1)} %get-tuple-element.526, f32[8,512,2048]{2,1,0:T(8,128)} %get-tuple-element.491, f32[8,512]{1,0:T(8,128)S(1)} %fusion.303, f32[8,512]{1,0:T(8,128)S(1)} %get-tuple-element.492, pred[2048]{0:T(1024)(128)(4,1)S(1)} %broadcast_in_dim.230), kind=kOutput, calls=%fused_computation.8.clone.1 | convolution fusion | flops 578945024 | bytes 34899968 | tf_op jit(solution)/shard_map/while/body/eval_jaxpr/hqk,khd->qhd/dot_general | solution.py:142
  278.4 14.2 fusion.302
  292.7 14.5 fusion.303
  307.2 15.4 %fusion.304 = bf16[8,512,32]{1,2,0:T(8,128)(2,1)} fusion(bf16[2048,8,32]{0,2,1:T(8,128)(2,1)} %get-tuple-element.526, f32[8,512,2048]{2,1,0:T(8,128)} %get-tuple-element.491, f32[8,512]{1,0:T(8,128)S(1)} %fusion.303, f32[8,512]{1,0:T(8,128)S(1)} %get-tuple-element.492, pred[2048]{0:T(1024)(128)(4,1)S(1)} %broadcast_in_dim.230), kind=kOutput, calls=%fused_computation.8.clone.1 | convolution fusion | flops 578945024 | bytes 34899968 | tf_op jit(solution)/shard_map/while/body/eval_jaxpr/hqk,khd->qhd/dot_general | solution.py:142
  326.8 14.2 fusion.302
  341.0 14.5 fusion.303
  355.5 15.4 %fusion.304 = bf16[8,512,32]{1,2,0:T(8,128)(2,1)} fusion(bf16[2048,8,32]{0,2,1:T(8,128)(2,1)} %get-tuple-element.526, f32[8,512,2048]{2,1,0:T(8,128)} %get-tuple-element.491, f32[8,512]{1,0:T(8,128)S(1)} %fusion.303, f32[8,512]{1,0:T(8,128)S(1)} %get-tuple-element.492, pred[2048]{0:T(1024)(128)(4,1)S(1)} %broadcast_in_dim.230), kind=kOutput, calls=%fused_computation.8.clone.1 | convolution fusion | flops 578945024 | bytes 34899968 | tf_op jit(solution)/shard_map/while/body/eval_jaxpr/hqk,khd->qhd/dot_general | solution.py:142
  379.9 21.7 %multiply_convert_fusion.1 = (bf16[2048,1024]{1,0:T(8,128)(2,1)S(1)}, f32[2048,1024]{1,0:T(8,128)}, f32[2048,1024]{1,0:T(8,128)}) fusion(f32[1024]{0:T(1024)S(1)} %copy-done.136, bf16[256,2048]{1,0:T(8,128)(2,1)S(1)} %copy-done.68, f32[2048,256]{1,0:T(8,128)S(1)} %get-tuple-element.380, f32[256]{0:T(256)S(1)} %copy-done.144, f32[256]{0:T(256)S(1)} %copy-done.138, ...), kind=kOutput, calls=%fused_computation.45 | convolution fusion | flops 1214775296 | bytes 23615488 | tf_op jit(solution)/shard_map/dot_general | solution.py:37
  406.5 10.7 copy.158
  417.3 11.6 copy.229
  441.0 24.5 %reshape.512 = f32[128,16,9,256]{3,2,1,0:T(8,128)} reshape(f32[2048,2304]{1,0:T(8,128)} %fusion.192) | data formatting | bytes 37748736 | tf_op jit(solution)/shard_map/reshape | solution.py:61
  465.5 56.6 %fusion.232 = (f32[128,16,1,256]{3,2,1,0:T(1,128)}, f32[128,16,1,256]{3,2,1,0:T(1,128)}, f32[128,16,1,256]{3,2,1,0:T(1,128)}, f32[128,16,1,256]{3,2,1,0:T(1,128)...) fusion(f32[128,16,9,256]{3,2,1,0:T(8,128)} %reshape.512), kind=kLoop, calls=%fused_computation.476 | loop fusion | bytes 37748736 | tf_op jit(solution)/shard_map/slice | solution.py:65
  569.9 405.6 %while.29 = (s32[]{:T(128)}, f32[2048,8,32]{0,2,1:T(8,128)}, f32[2048,8,32]{0,2,1:T(8,128)}, bf16[4,512,8,32]{1,3,2,0:T(8,128)(2,1)}, bf16[4,512,8,32]{1,3,2,0:T...) while((s32[]{:T(128)}, f32[2048,8,32]{0,2,1:T(8,128)}, ...), condition=%wide.region_25.26_spmd.clone, body=%wide.region_23.25_spmd.clone.sunk | while | flops 2770333696 | bytes 331964736 | solution.py:181
  571.2 17.0 %fusion.314 = f32[8,512,2048]{2,1,0:T(8,128)} fusion(bf16[2048,8,32]{0,2,1:T(8,128)(2,1)} %get-tuple-element.561, bf16[4,512,8,32]{1,3,2,0:T(8,128)(2,1)} %get-tuple-element.560, s32[]{:T(128)S(6)} %copy.319), kind=kOutput, calls=%fused_computation.29.clone.1 | convolution fusion | flops 536870912 | bytes 34865156 | tf_op jit(solution)/shard_map/while/body/eval_jaxpr/qhd,khd->hqk/dot_general | solution.py:161
  588.2 23.9 %multiply_reduce_fusion.29 = (f32[8,512]{1,0:T(8,128)S(1)}, f32[8,512,2048]{2,1,0:T(8,128)}) fusion(f32[8,512,2048]{2,1,0:T(8,128)} %fusion.314, f32[8,512]{1,0:T(8,128)S(1)} %dynamic-slice_bitcast_fusion.2, bf16[2048,8,32]{0,2,1:T(8,128)(2,1)S(1)} %get-tuple-element.558, bf16[4,512,8,32]{1,3,2,0:T(8,128)(2,1)} %get-tuple-element.557, ...), kind=kOutput, calls=%fused_computation.18.clone.1 | convolution fusion | flops 578809856 | bytes 68454400 | tf_op jit(solution)/shard_map/while/body/eval_jaxpr/qhd,khd->hqk/dot_general | solution.py:127
  612.1 27.5 %multiply_convert_fusion.6 = bf16[8,512,2048]{2,1,0:T(8,128)(2,1)} fusion(f32[8,512,2048]{2,1,0:T(8,128)} %fusion.314, f32[8,512,2048]{2,1,0:T(8,128)} %get-tuple-element.503, f32[8,512]{1,0:T(8,128)S(1)} %get-tuple-element.504), kind=kLoop, calls=%fused_computation.17.clone.1 | loop fusion | flops 33554432 | bytes 83902464 | tf_op jit(solution)/shard_map/while/body/eval_jaxpr/convert_element_type | solution.py:165
  639.6 14.9 %fusion.316 = f32[2048,8,32]{0,2,1:T(8,128)} fusion(f32[8,512,2048]{2,1,0:T(8,128)} %get-tuple-element.503, f32[2048,8,32]{0,2,1:T(8,128)} %get-tuple-element.543, pred[]{:T(512)S(6)} %compare.39, bf16[4,512,8,32]{1,3,2,0:T(8,128)(2,1)} %get-tuple-element.560, s32[]{:T(128)S(6)} %copy.319), kind=kOutput, calls=%fused_computation.25.clone.1 | convolution fusion | flops 546308096 | bytes 38010884 | tf_op jit(solution)/shard_map/while/body/eval_jaxpr/hqk,qhd->khd/dot_general | solution.py:172
  671.5 16.9 %fusion.314 = f32[8,512,2048]{2,1,0:T(8,128)} fusion(bf16[2048,8,32]{0,2,1:T(8,128)(2,1)} %get-tuple-element.561, bf16[4,512,8,32]{1,3,2,0:T(8,128)(2,1)} %get-tuple-element.560, s32[]{:T(128)S(6)} %copy.319), kind=kOutput, calls=%fused_computation.29.clone.1 | convolution fusion | flops 536870912 | bytes 34865156 | tf_op jit(solution)/shard_map/while/body/eval_jaxpr/qhd,khd->hqk/dot_general | solution.py:161
  688.4 23.9 %multiply_reduce_fusion.29 = (f32[8,512]{1,0:T(8,128)S(1)}, f32[8,512,2048]{2,1,0:T(8,128)}) fusion(f32[8,512,2048]{2,1,0:T(8,128)} %fusion.314, f32[8,512]{1,0:T(8,128)S(1)} %dynamic-slice_bitcast_fusion.2, bf16[2048,8,32]{0,2,1:T(8,128)(2,1)S(1)} %get-tuple-element.558, bf16[4,512,8,32]{1,3,2,0:T(8,128)(2,1)} %get-tuple-element.557, ...), kind=kOutput, calls=%fused_computation.18.clone.1 | convolution fusion | flops 578809856 | bytes 68454400 | tf_op jit(solution)/shard_map/while/body/eval_jaxpr/qhd,khd->hqk/dot_general | solution.py:127
  712.3 27.5 %multiply_convert_fusion.6 = bf16[8,512,2048]{2,1,0:T(8,128)(2,1)} fusion(f32[8,512,2048]{2,1,0:T(8,128)} %fusion.314, f32[8,512,2048]{2,1,0:T(8,128)} %get-tuple-element.503, f32[8,512]{1,0:T(8,128)S(1)} %get-tuple-element.504), kind=kLoop, calls=%fused_computation.17.clone.1 | loop fusion | flops 33554432 | bytes 83902464 | tf_op jit(solution)/shard_map/while/body/eval_jaxpr/convert_element_type | solution.py:165
  739.8 15.6 %fusion.316 = f32[2048,8,32]{0,2,1:T(8,128)} fusion(f32[8,512,2048]{2,1,0:T(8,128)} %get-tuple-element.503, f32[2048,8,32]{0,2,1:T(8,128)} %get-tuple-element.543, pred[]{:T(512)S(6)} %compare.39, bf16[4,512,8,32]{1,3,2,0:T(8,128)(2,1)} %get-tuple-element.560, s32[]{:T(128)S(6)} %copy.319), kind=kOutput, calls=%fused_computation.25.clone.1 | convolution fusion | flops 546308096 | bytes 38010884 | tf_op jit(solution)/shard_map/while/body/eval_jaxpr/hqk,qhd->khd/dot_general | solution.py:172
  773.0 16.9 %fusion.314 = f32[8,512,2048]{2,1,0:T(8,128)} fusion(bf16[2048,8,32]{0,2,1:T(8,128)(2,1)} %get-tuple-element.561, bf16[4,512,8,32]{1,3,2,0:T(8,128)(2,1)} %get-tuple-element.560, s32[]{:T(128)S(6)} %copy.319), kind=kOutput, calls=%fused_computation.29.clone.1 | convolution fusion | flops 536870912 | bytes 34865156 | tf_op jit(solution)/shard_map/while/body/eval_jaxpr/qhd,khd->hqk/dot_general | solution.py:161
  790.0 23.9 %multiply_reduce_fusion.29 = (f32[8,512]{1,0:T(8,128)S(1)}, f32[8,512,2048]{2,1,0:T(8,128)}) fusion(f32[8,512,2048]{2,1,0:T(8,128)} %fusion.314, f32[8,512]{1,0:T(8,128)S(1)} %dynamic-slice_bitcast_fusion.2, bf16[2048,8,32]{0,2,1:T(8,128)(2,1)S(1)} %get-tuple-element.558, bf16[4,512,8,32]{1,3,2,0:T(8,128)(2,1)} %get-tuple-element.557, ...), kind=kOutput, calls=%fused_computation.18.clone.1 | convolution fusion | flops 578809856 | bytes 68454400 | tf_op jit(solution)/shard_map/while/body/eval_jaxpr/qhd,khd->hqk/dot_general | solution.py:127
  813.9 27.5 %multiply_convert_fusion.6 = bf16[8,512,2048]{2,1,0:T(8,128)(2,1)} fusion(f32[8,512,2048]{2,1,0:T(8,128)} %fusion.314, f32[8,512,2048]{2,1,0:T(8,128)} %get-tuple-element.503, f32[8,512]{1,0:T(8,128)S(1)} %get-tuple-element.504), kind=kLoop, calls=%fused_computation.17.clone.1 | loop fusion | flops 33554432 | bytes 83902464 | tf_op jit(solution)/shard_map/while/body/eval_jaxpr/convert_element_type | solution.py:165
  841.4 15.6 %fusion.316 = f32[2048,8,32]{0,2,1:T(8,128)} fusion(f32[8,512,2048]{2,1,0:T(8,128)} %get-tuple-element.503, f32[2048,8,32]{0,2,1:T(8,128)} %get-tuple-element.543, pred[]{:T(512)S(6)} %compare.39, bf16[4,512,8,32]{1,3,2,0:T(8,128)(2,1)} %get-tuple-element.560, s32[]{:T(128)S(6)} %copy.319), kind=kOutput, calls=%fused_computation.25.clone.1 | convolution fusion | flops 546308096 | bytes 38010884 | tf_op jit(solution)/shard_map/while/body/eval_jaxpr/hqk,qhd->khd/dot_general | solution.py:172
  874.6 16.9 %fusion.314 = f32[8,512,2048]{2,1,0:T(8,128)} fusion(bf16[2048,8,32]{0,2,1:T(8,128)(2,1)} %get-tuple-element.561, bf16[4,512,8,32]{1,3,2,0:T(8,128)(2,1)} %get-tuple-element.560, s32[]{:T(128)S(6)} %copy.319), kind=kOutput, calls=%fused_computation.29.clone.1 | convolution fusion | flops 536870912 | bytes 34865156 | tf_op jit(solution)/shard_map/while/body/eval_jaxpr/qhd,khd->hqk/dot_general | solution.py:161
  891.6 23.9 %multiply_reduce_fusion.29 = (f32[8,512]{1,0:T(8,128)S(1)}, f32[8,512,2048]{2,1,0:T(8,128)}) fusion(f32[8,512,2048]{2,1,0:T(8,128)} %fusion.314, f32[8,512]{1,0:T(8,128)S(1)} %dynamic-slice_bitcast_fusion.2, bf16[2048,8,32]{0,2,1:T(8,128)(2,1)S(1)} %get-tuple-element.558, bf16[4,512,8,32]{1,3,2,0:T(8,128)(2,1)} %get-tuple-element.557, ...), kind=kOutput, calls=%fused_computation.18.clone.1 | convolution fusion | flops 578809856 | bytes 68454400 | tf_op jit(solution)/shard_map/while/body/eval_jaxpr/qhd,khd->hqk/dot_general | solution.py:127
  915.5 27.5 %multiply_convert_fusion.6 = bf16[8,512,2048]{2,1,0:T(8,128)(2,1)} fusion(f32[8,512,2048]{2,1,0:T(8,128)} %fusion.314, f32[8,512,2048]{2,1,0:T(8,128)} %get-tuple-element.503, f32[8,512]{1,0:T(8,128)S(1)} %get-tuple-element.504), kind=kLoop, calls=%fused_computation.17.clone.1 | loop fusion | flops 33554432 | bytes 83902464 | tf_op jit(solution)/shard_map/while/body/eval_jaxpr/convert_element_type | solution.py:165
  943.0 15.6 %fusion.316 = f32[2048,8,32]{0,2,1:T(8,128)} fusion(f32[8,512,2048]{2,1,0:T(8,128)} %get-tuple-element.503, f32[2048,8,32]{0,2,1:T(8,128)} %get-tuple-element.543, pred[]{:T(512)S(6)} %compare.39, bf16[4,512,8,32]{1,3,2,0:T(8,128)(2,1)} %get-tuple-element.560, s32[]{:T(128)S(6)} %copy.319), kind=kOutput, calls=%fused_computation.25.clone.1 | convolution fusion | flops 546308096 | bytes 38010884 | tf_op jit(solution)/shard_map/while/body/eval_jaxpr/hqk,qhd->khd/dot_general | solution.py:172
  1104.5 29.7 %reduce-scatter.5.cloned.1.call-done = f32[3,64,512]{2,1,0:T(8,128)} async-done(((f32[3,512,512]{2,1,0:T(8,128)}), f32[3,64,512]{2,1,0:T(8,128)}) %reduce-scatter.5.cloned.1.call-update) | async-done | bytes 393232 | tf_op jit(solution)/shard_map/reduce_scatter | solution.py:380
  1135.9 54.6 %reduce-scatter.7.cloned.1.call-done = f32[2,288,256]{2,1,0:T(8,128)} async-done(((f32[2,2304,256]{2,1,0:T(8,128)}), f32[2,288,256]{2,1,0:T(8,128)}) %reduce-scatter.7.cloned.1.call-update) | async-done | bytes 589840 | tf_op jit(solution)/shard_map/reduce_scatter | solution.py:381
  1192.5 38.6 %all-reduce.36 = (f32[]{:T(128)}, f32[5896]{0:T(1024)S(1)}) all-reduce(f32[]{:T(128)} %get-tuple-element.242, f32[5896]{0:T(1024)S(1)} %constant_dynamic-update-slice_fusion.14), channel_id=1, replica_groups=mesh['dp'=4,'fsdp'=8] {'dp','fsdp'}, use_global_device_ids=true, to_apply=%region_18.19 | all-reduce | flops 5897 | bytes 47176 | tf_op jit(solution)/shard_map/psum | solution.py:397
  1232.3 83.9 %all-reduce.42.cloned.1.call-done = (f32[72,256]{1,0:T(8,128)}, f32[2304,8]{0,1:T(8,128)}) async-done(((f32[72,256]{1,0:T(8,128)}, f32[2304,8]{0,1:T(8,128)}), (f32[72,256]{1,0:T(8,128)}, f32[2304,8]{0,1:T(8,128)})) %all-reduce.42.cloned.1.call-update) | async-done | bytes 147472 | tf_op jit(solution)/shard_map/psum | solution.py:397
  1320.6 51.0 %all-reduce.44.cloned.1.call-done = (bf16[3,64,512]{2,1,0:T(8,128)(2,1)}, bf16[2,288,256]{2,1,0:T(8,128)(2,1)}, bf16[32,2048]{1,0:T(8,128)(2,1)}, bf16[128,256]{1,0:T(8,128)(2,1)}) async-done(((bf16[3,64,512]{2,1,0:T(8,128)(2,1)}, bf16[2,288,256]{2,1,0:T(8,128)(2,1)}, bf16[32,2048]{1,0:T(8,128)(2,1)}, bf16[128,256]{1,0:T(8,128)(2,1)}), (bf16[3,64,512]{2,1,0:T(8,128)(2,1)}, bf16[2,288,256]{2,1,0:T(8,128)(2,1)}, ...) | async-done | bytes 688144 | tf_op jit(solution)/shard_map/psum | solution.py:386
  1381.2 17.2 %psum.76 = f32[]{:T(128)} all-reduce(f32[]{:T(128)S(6)} %add.609), channel_id=1, replica_groups=mesh['dp'=4,'fsdp'=8] {'fsdp'}, use_global_device_ids=true, to_apply=%region_49.50 | all-reduce | flops 1 | bytes 8 | tf_op jit(solution)/shard_map/psum | solution.py:400
  1443.1 10.5 all-to-all-done.3
  1462.1 10.3 all-to-all-done.2
  (632 shorter events, 427.6 us)
Async XLA Ops:
  7.2 1404.8 %copy-start = (f32[768,768]{1,0:T(8,128)S(1)}, f32[768,768]{1,0:T(8,128)}, u32[]{:S(2)}) copy-start(f32[768,768]{1,0:T(8,128)} %param.46) | copy-start | bytes 7077892
  7.2 53.2 %copy-start.63 = (f32[128,256]{1,0:T(8,128)S(1)}, f32[128,256]{1,0:T(8,128)}, u32[]{:S(2)}) copy-start(f32[128,256]{1,0:T(8,128)} %param.44) | copy-start | bytes 393220
  7.2 53.3 %copy-start.72 = (bf16[1,128,16,8]{1,3,2,0:T(8,128)(2,1)S(1)}, bf16[1,128,16,8]{1,3,2,0:T(8,128)(2,1)}, u32[]{:S(2)}) copy-start(bf16[1,128,16,8]{1,3,2,0:T(8,128)(2,1)} %param.33) | copy-start | bytes 98308
  7.2 53.4 %copy-start.77 = (bf16[1,128,16,8]{1,3,2,0:T(8,128)(2,1)S(1)}, bf16[1,128,16,8]{1,3,2,0:T(8,128)(2,1)}, u32[]{:S(2)}) copy-start(bf16[1,128,16,8]{1,3,2,0:T(8,128)(2,1)} %param.32) | copy-start | bytes 98308
  7.3 109.5 %all-gather.4.cloned.1.call-start = ((), (), s32[]{:S(2)}) async-start(), calls=%async_computation.8 | async-start | bytes 2654208 | tf_op jit(solution)/shard_map/all_gather | solution.py:253
  9.3 110.6 %all-gather.6.cloned.1.call-start = ((), (), s32[]{:S(2)}) async-start(), calls=%async_computation.9 | async-start | bytes 3538944 | tf_op jit(solution)/shard_map/all_gather | solution.py:251
  10.0 161.1 %all-gather.8.cloned.1.call-start = ((), (), s32[]{:S(2)}) async-start(), calls=%async_computation.10 | async-start | bytes 1179648 | tf_op jit(solution)/shard_map/all_gather | solution.py:254
  11.7 1089.6 %reduce-scatter.11.cloned.1.call-start = ((), (), s32[]{:S(2)}) async-start(), calls=%async_computation.14 | async-start | bytes 1179648 | tf_op jit(solution)/shard_map/reduce_scatter | solution.py:383
  13.6 78.6 %copy-start.120 = (f32[256]{0:T(256)}, f32[256]{0:T(256)S(1)}, u32[]{:S(2)}) copy-start(f32[256]{0:T(256)S(1)} %get-tuple-element.369) | copy-start | bytes 3076
  13.6 78.7 %copy-start.122 = (f32[256]{0:T(256)}, f32[256]{0:T(256)S(1)}, u32[]{:S(2)}) copy-start(f32[256]{0:T(256)S(1)} %get-tuple-element.370) | copy-start | bytes 3076
  13.6 123.7 %copy-start.124 = (f32[256]{0:T(256)}, f32[256]{0:T(256)S(1)}, u32[]{:S(2)}) copy-start(f32[256]{0:T(256)S(1)} %get-tuple-element.366) | copy-start | bytes 3076
  13.6 123.7 %copy-start.126 = (f32[256]{0:T(256)}, f32[256]{0:T(256)S(1)}, u32[]{:S(2)}) copy-start(f32[256]{0:T(256)S(1)} %get-tuple-element.367) | copy-start | bytes 3076
  13.6 157.5 %copy-start.118 = (f32[256]{0:T(256)}, f32[256]{0:T(256)S(1)}, u32[]{:S(2)}) copy-start(f32[256]{0:T(256)S(1)} %get-tuple-element.364) | copy-start | bytes 3076
  13.6 157.5 %copy-start.132 = (f32[256]{0:T(256)}, f32[256]{0:T(256)S(1)}, u32[]{:S(2)}) copy-start(f32[256]{0:T(256)S(1)} %get-tuple-element.363) | copy-start | bytes 3076
  15.2 66.9 %copy-start.99 = (f32[128]{0:T(128)}, f32[128]{0:T(128)S(1)}, u32[]{:S(2)}) copy-start(f32[128]{0:T(128)S(1)} %fusion.211) | copy-start | bytes 1540
  60.5 76.9 %copy-start.47 = (f32[2048]{0:T(1024)}, f32[2048]{0:T(1024)S(1)}, u32[]{:S(2)}) copy-start(f32[2048]{0:T(1024)S(1)} %broadcast_in_dim.145) | copy-start | bytes 24580
  121.9 12.1 copy-start.102
  153.2 11.7 copy-start.6
  181.4 193.5 %copy-start.134 = (f32[256]{0:T(256)S(1)}, f32[256]{0:T(256)}, u32[]{:S(2)}) copy-start(f32[256]{0:T(256)} %get-tuple-element.362) | copy-start | bytes 3076
  377.8 23.8 %copy-start.15 = (f32[2048,256]{1,0:T(8,128)}, f32[2048,256]{1,0:T(8,128)S(1)}, u32[]{:S(2)}) copy-start(f32[2048,256]{1,0:T(8,128)S(1)} %get-tuple-element.380) | copy-start | bytes 6291460
  377.9 180.6 %copy-start.78 = (f32[2048]{0:T(1024)}, f32[2048]{0:T(1024)S(1)}, u32[]{:S(2)}) copy-start(f32[2048]{0:T(1024)S(1)} %broadcast_multiply_fusion.3) | copy-start | bytes 24580
  378.6 23.1 %copy-start.86 = (f32[2048]{0:T(1024)}, f32[2048]{0:T(1024)S(1)}, u32[]{:S(2)}) copy-start(f32[2048]{0:T(1024)S(1)} %multiply_reduce_fusion.13) | copy-start | bytes 24580
  378.6 179.9 %copy-start.94 = (f32[2048]{0:T(1024)}, f32[2048]{0:T(1024)S(1)}, u32[]{:S(2)}) copy-start(f32[2048]{0:T(1024)S(1)} %fusion.196) | copy-start | bytes 24580
  379.9 21.8 %copy-start.48 = (f32[2048]{0:T(1024)S(1)}, f32[2048]{0:T(1024)}, u32[]{:S(2)}) copy-start(f32[2048]{0:T(1024)} %copy-done.47) | copy-start | bytes 24580
  379.9 21.8 %copy-start.65 = (bf16[1024,256]{1,0:T(8,128)(2,1)S(1)}, bf16[1024,256]{1,0:T(8,128)(2,1)}, u32[]{:S(2)}) copy-start(bf16[1024,256]{1,0:T(8,128)(2,1)} %all_gather.18) | copy-start | bytes 1572868
  379.9 21.8 %copy-start.146 = (f32[256]{0:T(256)S(1)}, f32[256]{0:T(256)}, u32[]{:S(2)}) copy-start(f32[256]{0:T(256)} %get-tuple-element.359) | copy-start | bytes 3076
  417.2 11.7 copy-start.59
  417.2 11.7 copy-start.70
  417.3 11.7 copy-start.130
  545.7 557.2 %reduce-scatter.9.cloned.1.call-start = ((), (), s32[]{:S(2)}) async-start(), calls=%async_computation.13 | async-start | bytes 2359296 | tf_op jit(solution)/shard_map/reduce_scatter | solution.py:382
  1056.9 77.3 %reduce-scatter.5.cloned.1.call-start = ((), (), s32[]{:S(2)}) async-start(), calls=%async_computation.11 | async-start | bytes 3538944 | tf_op jit(solution)/shard_map/reduce_scatter | solution.py:380
  1071.3 119.2 %reduce-scatter.7.cloned.1.call-start = ((), (), s32[]{:S(2)}) async-start(), calls=%async_computation.12 | async-start | bytes 5308416 | tf_op jit(solution)/shard_map/reduce_scatter | solution.py:381
  1085.7 230.5 %all-reduce.42.cloned.1.call-start = ((), (), s32[]{:S(2)}) async-start(), calls=%async_computation.15 | async-start | bytes 294912 | tf_op jit(solution)/shard_map/psum | solution.py:397
  1094.6 277.0 %all-reduce.44.cloned.1.call-start = ((), (), s32[]{:S(2)}) async-start(), calls=%async_computation.16 | async-start | bytes 1376256 | tf_op jit(solution)/shard_map/psum | solution.py:386
  1101.3 91.1 %copy-start.135 = (f32[1024]{0:T(1024)S(1)}, f32[1024]{0:T(1024)}, u32[]{:S(2)}) copy-start(f32[1024]{0:T(1024)} %get-tuple-element.385) | copy-start | bytes 12292
  1101.3 91.1 %copy-start.147 = (f32[8]{0:T(128)S(1)}, f32[8]{0:T(128)}, u32[]{:S(2)}) copy-start(f32[8]{0:T(128)} %get-tuple-element.241) | copy-start | bytes 100
  1231.1 168.1 %copy-start.80 = (f32[5896]{0:T(1024)}, f32[5896]{0:T(1024)S(1)}, u32[]{:S(2)}) copy-start(f32[5896]{0:T(1024)S(1)} %get-tuple-element.278) | copy-start | bytes 70756
  1400.3 11.7 copy-start.52
  1408.0 10.8 all-to-all-start.1
  1413.5 12.9 copy-start.45
  1416.9 12.0 copy-start.66
  1418.8 15.9 %all-to-all-start = ((bf16[8,32,768]{2,1,0:T(8,128)(2,1)}), bf16[8,32,768]{2,1,0:T(8,128)(2,1)S(1)}, u32[]{:S(2)}, u32[]{:S(2)}) async-start(bf16[8,32,768]{2,1,0:T(8,128)(2,1)} %bitcast.540), calls=%async_computation.4 | async-start | bytes 786432 | tf_op jit(solution)/shard_map/all_to_all | solution.py:32
  1426.4 15.0 %copy-start.60 = (f32[2304,8]{0,1:T(8,128)S(1)}, f32[2304,8]{0,1:T(8,128)}, u32[]{:S(2)}) copy-start(f32[2304,8]{0,1:T(8,128)} %param.39) | copy-start | bytes 221188
  1434.7 18.9 %copy-start.50 = (bf16[8,32,768]{2,1,0:T(8,128)(2,1)}, bf16[8,32,768]{2,1,0:T(8,128)(2,1)S(1)}, u32[]{:S(2)}) copy-start(bf16[8,32,768]{2,1,0:T(8,128)(2,1)S(1)} %all-to-all-done) | copy-start | bytes 1179652
  1434.7 22.4 %copy-start.98 = (f32[5896]{0:T(1024)S(1)}, f32[5896]{0:T(1024)}, u32[]{:S(2)}) copy-start(f32[5896]{0:T(1024)} %param.54) | copy-start | bytes 70756
  1434.7 18.9 %all-to-all-start.3 = ((bf16[8,128,256]{2,1,0:T(8,128)(2,1)}), bf16[8,128,256]{2,1,0:T(8,128)(2,1)S(1)}, u32[]{:S(2)}, u32[]{:S(2)}) async-start(bf16[8,128,256]{2,1,0:T(8,128)(2,1)} %bitcast.121), calls=%async_computation.7 | async-start | bytes 1048576 | tf_op jit(solution)/shard_map/all_to_all | solution.py:32
  1441.4 18.9 %copy-start.81 = (f32[5896]{0:T(1024)}, f32[5896]{0:T(1024)S(1)}, u32[]{:S(2)}) copy-start(f32[5896]{0:T(1024)S(1)} %get-tuple-element.289) | copy-start | bytes 70756
  1453.6 18.8 %all-to-all-start.2 = ((bf16[8,32,1024]{2,1,0:T(8,128)(2,1)}), bf16[8,32,1024]{2,1,0:T(8,128)(2,1)S(1)}, u32[]{:S(2)}, u32[]{:S(2)}) async-start(bf16[8,32,1024]{2,1,0:T(8,128)(2,1)} %bitcast.539), calls=%async_computation.6 | async-start | bytes 1048576 | tf_op jit(solution)/shard_map/all_to_all | solution.py:32
  (120 other events, 427.5 us)
Sparse Core Ops, SparseCore 0:
  10.3 35.0 all-gather.3
  46.9 41.5 all-gather.5
  90.7 20.9 all-gather.7
  545.8 32.6 reduce-scatter.10
  1057.1 36.0 reduce-scatter.8
  1095.3 38.8 reduce-scatter.4
  1136.5 53.9 reduce-scatter.6
  1196.8 119.4 all-reduce.41
  1321.3 50.2 all-reduce.43
where the time goes:
time: 1500 us; the launch traced here: 1480 us
  matrix products  542 us (36%)
  local copies, waits for them, and re-layouts  274 us (18%)
  other arithmetic  258 us (17%)
  waiting for transfers between devices  249 us (17%)
  blocking collectives  117 us (8%)
  between operations  28.3 us (2%)
  starting transfers between devices  15.3 us (1%)
    dot_general x8, matrix products, block_scores(): jnp.einsum('qhd,khd->hqk', query_block, key_heads, preferred_element_type...  153 us
    convert_element_type x4, other arithmetic, one_block(): (factor * soft_weights * (grad_soft - weighted)).astype(jnp.bfloat16)  110 us
    psum x1, waiting for transfers between devices, local(): lax.psum((loss_local, grad_stem_w, grad_head_w, grad_vector), ('dp', 'fsd...  83.9 us
    unnamed x363, local copies, waits for them, and re-layouts  79.4 us
    dot_general x4, matrix products, one_block(): jnp.einsum('qhd,khd->hqk', grad_block, value_heads, preferred_element_typ...  67.7 us
    dot_general x4, matrix products, one_block(): jnp.einsum('hqk,qhd->khd', soft_weights.astype(jnp.bfloat16), grad_block,...  61.6 us
    dot_general x4, matrix products, one_block(): jnp.einsum('hqk,khd->qhd', soft_weights, value_heads, preferred_element_t...  61.5 us
    reduce_sum x4, other arithmetic, one_block(): denominator = jnp.sum(lifted, axis=-1, keepdims=True)  57.9 us
  transfers between devices with their start and end apart: 13, of which 8 were waited for; matrix products, arithmetic and copies ran while one was open for 45% of the time, Pallas kernels for 0%

commit v1 on v0

v1 whole, which is shorter than its diff:
```python
import functools
import math

import jax
import jax.numpy as jnp
from jax import lax
from jax.experimental import pallas as pl
from jax.experimental.pallas import tpu as pltpu
from jax.sharding import PartitionSpec as P

HEADS = 8
FF = 1024
EMB = 512
GROUPS = 32

norm_floor = 1e-05
masked_score = -1e30
clip_limit = 0.002
adam_rate = 0.05
adam_floor = 1e-08
shampoo_rate = 0.02
decay_rate = 0.01

f32 = jnp.float32
bf16 = jnp.bfloat16
highest = lax.Precision.HIGHEST
LOG2E = math.log2(math.e)
CHUNK = 256


def mm(left_op, right_op):
    return jnp.dot(left_op, right_op, preferred_element_type=f32)


def mm_nt(left_op, right_op):
    return lax.dot_general(
        left_op, right_op, (((1,), (1,)), ((), ())), preferred_element_type=f32
    )


def col_sum(value):
    return jnp.sum(value, axis=0, keepdims=True)


def row_mean(value):
    return jnp.mean(value, axis=-1, keepdims=True)


def loop(count, body, init):
    return lax.fori_loop(0, count, body, init)


def tap_shift(field, a, b, freq_bins):
    length = field.shape[1]
    step = freq_bins * (a - 1) + (b - 1)
    if step == 0:
        return field
    pos = lax.broadcasted_iota(jnp.int32, field.shape, 1)
    bin_pos = lax.rem(pos, freq_bins)
    keep = None
    for wanted, test in (
        (a == 0, lambda: pos >= freq_bins),
        (a == 2, lambda: pos < length - freq_bins),
        (b == 0, lambda: bin_pos >= 1),
        (b == 2, lambda: bin_pos < freq_bins - 1),
    ):
        if wanted:
            keep = test() if keep is None else jnp.logical_and(keep, test())
    return jnp.where(keep, pltpu.roll(field, (-step) % length, 1), 0.0)


def put_shifted(buf, start, value, freq_bins):
    rows, channels = value.shape
    bin_pos = lax.rem(lax.broadcasted_iota(jnp.int32, value.shape, 0), freq_bins)
    before = jnp.where(bin_pos == 0, 0.0, pltpu.roll(value, 1, 0))
    after = jnp.where(bin_pos == freq_bins - 1, 0.0, pltpu.roll(value, rows - 1, 0))
    where = pl.ds(start + freq_bins, rows)
    buf[where, 0:channels] = before.astype(bf16)
    buf[where, channels : 2 * channels] = value.astype(bf16)
    buf[where, 2 * channels : 3 * channels] = after.astype(bf16)


def clear_ends(buf, rows_n, freq_bins):
    blank = jnp.zeros((freq_bins, buf.shape[1]), bf16)
    buf[0:freq_bins, :] = blank
    buf[rows_n + freq_bins : rows_n + 2 * freq_bins, :] = blank


def live_rows(start, shape, live):
    return start + lax.broadcasted_iota(jnp.int32, shape, 0) < live


def group_total(row, groups):
    channels = row.shape[1]
    size = channels // groups
    one = lax.broadcasted_iota(jnp.int32, (channels, channels), 0) // size
    two = lax.broadcasted_iota(jnp.int32, (channels, channels), 1) // size
    same = jnp.where(one == two, 1.0, 0.0).astype(f32)
    wide = jnp.broadcast_to(row, (8, channels))
    return jnp.dot(wide, same, precision=highest, preferred_element_type=f32)[0:1]


def vec_mat(row, weight, transposed=False):
    top = row.astype(bf16).astype(f32)
    rest = row - top
    mid = rest.astype(bf16).astype(f32)
    low = rest - mid
    shape = (16, row.shape[1])
    index = lax.broadcasted_iota(jnp.int32, shape, 0)
    stacked = jnp.where(
        index == 0,
        jnp.broadcast_to(top, shape),
        jnp.where(
            index == 1,
            jnp.broadcast_to(mid, shape),
            jnp.where(index == 2, jnp.broadcast_to(low, shape), 0.0),
        ),
    ).astype(bf16)
    return col_sum(mm_nt(stacked, weight) if transposed else mm(stacked, weight))


def silu_slope(value):
    gate = jax.nn.sigmoid(value)
    return gate * (1.0 + value * (1.0 - gate))


def group_stats(read, rows_n, live, channels, groups, counted):
    count = rows_n // CHUNK

    def add(i, total):
        start = pl.multiple_of(i * CHUNK, CHUNK)
        value = read(start)
        return total + col_sum(jnp.where(live_rows(start, value.shape, live), value, 0.0))

    center = group_total(loop(count, add, jnp.zeros((1, channels), f32)), groups) / counted

    def add_square(i, total):
        start = pl.multiple_of(i * CHUNK, CHUNK)
        value = read(start) - center
        return total + col_sum(jnp.where(live_rows(start, value.shape, live), value * value, 0.0))

    spread = group_total(loop(count, add_square, jnp.zeros((1, channels), f32)), groups) / counted
    return center, lax.rsqrt(spread + norm_floor)


def offsets(channels, embed_width, hidden_units, latent_ch):
    starts = []
    start = 0
    for length in [channels] * 13 + [embed_width] * 3 + [hidden_units, latent_ch]:
        starts.append((start, length))
        start = start + length
    return starts


def fore_kernel(
    freq_bins,
    groups,
    len_ref,
    mix_ref,
    lat_ref,
    noi_ref,
    stem_ref,
    conv_ref,
    wide_ref,
    time_ref,
    vec_ref,
    wave_ref,
    clap_ref,
    zero_ref,
    act_one_ref,
    inner_ref,
    act_two_ref,
    one_ref,
    normed_ref,
    qkv_ref,
    colsT_ref,
    noiT_ref,
    stat_ref,
    film_ref,
    buf,
    cols,
    tall,
):
    rows_n, channels = zero_ref.shape
    latent_ch = lat_ref.shape[1]
    embed = time_ref.shape[1]
    count = rows_n // CHUNK
    live = len_ref[0] * freq_bins
    counted = (live * (channels // groups)).astype(f32)
    segs = offsets(channels, embed, FF, latent_ch)

    def seg(index):
        start, length = segs[index]
        return vec_ref[:, start : start + length]

    wave = wave_ref[...]
    pre_time = vec_mat(wave, time_ref[0]) + seg(13)
    embedding = vec_mat(jax.nn.silu(pre_time), time_ref[1]) + seg(14) + clap_ref[...]
    film = vec_mat(jax.nn.silu(embedding), time_ref[2]) + seg(15)
    film_ref[0:1] = film
    film_ref[1:2] = pre_time
    film_ref[2:3] = embedding
    film_ref[3:8] = jnp.zeros((5, embed), f32)
    lift = 1.0 + film[:, :channels]
    move = film[:, channels:]

    eye = jnp.where(
        lax.broadcasted_iota(jnp.int32, (latent_ch, latent_ch), 0)
        == lax.broadcasted_iota(jnp.int32, (latent_ch, latent_ch), 1),
        1.0,
        0.0,
    ).astype(bf16)
    noise_t = mm_nt(eye, noi_ref[...])
    noiT_ref[...] = noise_t
    mixed = mix_ref[0] * mm_nt(eye, lat_ref[...]) + mix_ref[1] * noise_t
    pos = lax.broadcasted_iota(jnp.int32, mixed.shape, 1)
    noisy = jnp.where(pos < live, mixed, 0.0).astype(bf16).astype(f32)
    taps = 9 * latent_ch
    for a in range(3):
        for b in range(3):
            tap = 3 * a + b
            tall[tap * latent_ch : (tap + 1) * latent_ch] = tap_shift(noisy, a, b, freq_bins)
    tall[taps:] = jnp.zeros((tall.shape[0] - taps, rows_n), f32)
    colsT_ref[...] = tall[0:taps].astype(bf16)
    cols[...] = tall[...].T.astype(bf16)
    stem_low = jnp.concatenate(
        [stem_ref[...], jnp.zeros((cols.shape[1] - taps, channels), f32)], 0
    ).astype(bf16)
    stem_bias = seg(12)

    def stem_part(i, carry):
        rows = pl.ds(pl.multiple_of(i * CHUNK, CHUNK), CHUNK)
        zero_ref[rows, :] = mm(cols[rows, :], stem_low) + stem_bias
        return carry

    loop(count, stem_part, 0)

    clear_ends(buf, rows_n, freq_bins)

    def convolve(which, start):
        total = None
        for a in range(3):
            part = mm(
                buf[pl.ds(start + freq_bins * a, CHUNK), :],
                conv_ref[which, 3 * a * channels : 3 * (a + 1) * channels, :],
            )
            total = part if total is None else total + part
        return total

    def activate(read, center, scale, gain, shift, act_ref):
        factor = scale * gain

        def part(i, carry):
            start = pl.multiple_of(i * CHUNK, CHUNK)
            value = jax.nn.silu((read(start) - center) * factor + shift)
            value = jnp.where(live_rows(start, value.shape, live), value, 0.0)
            low = value.astype(bf16)
            act_ref[pl.ds(start, CHUNK), :] = low
            put_shifted(buf, start, low.astype(f32), freq_bins)
            return carry

        loop(count, part, 0)

    def read_zero(start):
        return zero_ref[pl.ds(start, CHUNK), :]

    center, scale = group_stats(read_zero, rows_n, live, channels, groups, counted)
    stat_ref[0:1] = center
    stat_ref[1:2] = scale
    activate(read_zero, center, scale, seg(0), seg(1), act_one_ref)

    bias_one = seg(2)

    def conv_part(i, carry):
        start = pl.multiple_of(i * CHUNK, CHUNK)
        inner_ref[pl.ds(start, CHUNK), :] = convolve(0, start) + bias_one
        return carry

    loop(count, conv_part, 0)

    def read_moved(start):
        return inner_ref[pl.ds(start, CHUNK), :] * lift + move

    center, scale = group_stats(read_moved, rows_n, live, channels, groups, counted)
    stat_ref[2:3] = center
    stat_ref[3:4] = scale
    stat_ref[4:8] = jnp.zeros((4, channels), f32)
    activate(read_moved, center, scale, seg(3), seg(4), act_two_ref)

    bias_two = seg(5)
    gain, shift = seg(6), seg(7)
    wqkv_t = wide_ref[...].T

    def last_part(i, carry):
        start = pl.multiple_of(i * CHUNK, CHUNK)
        rows = pl.ds(start, CHUNK)
        stream = zero_ref[rows, :] + convolve(1, start) + bias_two
        one_ref[rows, :] = stream
        gap = stream - row_mean(stream)
        normed = gap * lax.rsqrt(row_mean(gap * gap) + norm_floor) * gain + shift
        low = normed.astype(bf16)
        normed_ref[rows, :] = low
        qkv_ref[:, rows] = mm_nt(wqkv_t, low).astype(bf16)
        return carry

    loop(count, last_part, 0)


def fill_query(aug, query, factor, extra):
    dim, length = query.shape
    scaled = query.astype(f32) * (factor * LOG2E)
    high = scaled.astype(bf16)
    aug[0:dim] = high
    aug[dim : 2 * dim] = (scaled - high.astype(f32)).astype(bf16)
    index = lax.broadcasted_iota(jnp.int32, (16, length), 0)
    tile = jnp.where(index == 0, 1.0, 0.0)
    for place, row in enumerate(extra):
        tile = jnp.where(index == place + 1, jnp.broadcast_to(row, tile.shape), tile)
    aug[2 * dim : 2 * dim + 16] = tile.astype(bf16)
    aug[2 * dim + 16 :] = jnp.zeros((aug.shape[0] - 2 * dim - 16, length), bf16)


def fill_keys(aug, keys, live):
    dim, length = keys.shape
    rest = aug.shape[1] - 2 * dim
    index = lax.broadcasted_iota(jnp.int32, (rest, length), 0)
    pos = lax.broadcasted_iota(jnp.int32, (rest, length), 1)
    mask = jnp.where(pos < live, 0.0, masked_score)
    tile = jnp.where(index == 0, mask, jnp.where(index < 4, 1.0, 0.0))
    both = keys.astype(f32)
    aug[...] = jnp.concatenate([both, both, tile], 0).T.astype(bf16)


def three_parts(row):
    top = row.astype(bf16).astype(f32)
    rest = row - top
    mid = rest.astype(bf16).astype(f32)
    return top, mid, rest - mid


def attend_kernel(
    freq_bins, key_block, len_ref, q_ref, k_ref, v_ref, o_ref, lse_ref, kaug, qaug, vaug
):
    dim, length = q_ref.shape
    live = len_ref[0] * freq_bins
    fill_query(qaug, q_ref[...], dim ** (-0.5), ())
    fill_keys(kaug, k_ref[...], live)
    vaug[0:dim] = v_ref[...]
    index = lax.broadcasted_iota(jnp.int32, (16, length), 0)
    vaug[dim : dim + 16] = jnp.where(index == 0, 1.0, 0.0).astype(bf16)
    top = None
    for i in range(length // key_block):
        keys = slice(i * key_block, (i + 1) * key_block)
        scores = mm(kaug[keys, :], qaug[...])
        block_top = jnp.max(scores, axis=0, keepdims=True)
        new_top = block_top if top is None else jnp.maximum(top, block_top)
        weights = jnp.exp2(scores - new_top).astype(bf16)
        part = mm(vaug[:, keys], weights)
        total = part if top is None else total * jnp.exp2(top - new_top) + part
        top = new_top
    summed = total[dim : dim + 1]
    o_ref[...] = total[0:dim] / summed
    lse_ref[0] = top + jnp.log2(summed)


def attend_back_kernel(
    freq_bins,
    key_block,
    len_ref,
    q_ref,
    k_ref,
    v_ref,
    lse_ref,
    o_ref,
    do_ref,
    dq_ref,
    dk_ref,
    dv_ref,
    kaug,
    qaug,
    vaug,
    daug,
    acc,
):
    dim, length = q_ref.shape
    step = pl.program_id(1)
    factor = dim ** (-0.5)

    @pl.when(step == 0)
    def _():
        live = len_ref[0] * freq_bins
        fill_query(qaug, q_ref[...], factor, three_parts(-lse_ref[0]))
        fill_keys(kaug, k_ref[...], live)
        values = v_ref[...].astype(f32)
        rest = vaug.shape[1] - dim
        index = lax.broadcasted_iota(jnp.int32, (rest, length), 0)
        tile = jnp.where(index < 3, -1.0, 0.0)
        vaug[...] = jnp.concatenate([values, tile], 0).T.astype(bf16)
        back = do_ref[...]
        delta = col_sum(back.astype(f32) * o_ref[...])
        daug[0:dim] = back
        index = lax.broadcasted_iota(jnp.int32, (16, length), 0)
        tile = jnp.zeros((16, length), f32)
        for place, row in enumerate(three_parts(delta)):
            tile = jnp.where(index == place, jnp.broadcast_to(row, tile.shape), tile)
        daug[dim : dim + 16] = tile.astype(bf16)
        daug[dim + 16 :] = jnp.zeros((daug.shape[0] - dim - 16, length), bf16)
        acc[...] = jnp.zeros(acc.shape, f32)

    keys = pl.ds(pl.multiple_of(step * key_block, key_block), key_block)
    weights = jnp.exp2(mm(kaug[keys, :], qaug[...]))
    raw = (weights * mm(vaug[keys, :], daug[...])).astype(bf16)
    dv_ref[...] = mm_nt(do_ref[...], weights.astype(bf16)).astype(bf16)
    dk_ref[...] = (mm_nt(q_ref[...], raw) * factor).astype(bf16)
    acc[...] += mm(k_ref[:, keys], raw)

    @pl.when(step == pl.num_programs(1) - 1)
    def _():
        dq_ref[...] = (acc[...] * factor).astype(bf16)


def middle_kernel(
    freq_bins,
    len_ref,
    mixed_ref,
    one_ref,
    wide_ref,
    down_ref,
    vec_ref,
    head_ref,
    head_bias_ref,
    noiT_ref,
    two_grad_ref,
    do_ref,
    gdown_ref,
    gup_ref,
    gproj_ref,
    ghead_ref,
    gvec_ref,
    small_ref,
    hidden,
    slope,
    xhat,
    spread,
    three,
    prod,
    gcols,
    normed_t,
    three_t,
    gpre,
    glow,
):
    rows_n, channels = one_ref.shape
    units = down_ref.shape[0]
    latent_ch = noiT_ref.shape[0]
    count = rows_n // CHUNK
    live = len_ref[0] * freq_bins
    segs = offsets(channels, EMB, units, latent_ch)

    def seg(index):
        start, length = segs[index]
        return vec_ref[:, start : start + length]

    w_out = wide_ref[:, 3 * channels : 4 * channels]
    proj_bias, gain, shift, up_bias, down_bias = seg(8), seg(9), seg(10), seg(16), seg(11)

    def fore(i, carry):
        start = pl.multiple_of(i * CHUNK, CHUNK)
        rows = pl.ds(start, CHUNK)
        mixed = mixed_ref[:, rows].T.astype(bf16)
        stream = one_ref[rows, :] + mm(mixed, w_out) + proj_bias
        gap = stream - row_mean(stream)
        scale = lax.rsqrt(row_mean(gap * gap) + norm_floor)
        hat = gap * scale
        xhat[rows, :] = hat
        spread[rows, :] = jnp.broadcast_to(scale, (CHUNK, spread.shape[1]))
        normed = (hat * gain + shift).astype(bf16)
        normed_t[:, rows] = normed.T
        pre = mm(normed, wide_ref[:, 4 * channels :]) + up_bias
        phi = 0.5 * (1.0 + lax.erf(pre * (0.5**0.5)))
        slope[rows, :] = phi + pre * jnp.exp(-0.5 * pre * pre) * (0.5 / math.pi) ** 0.5
        low = (pre * phi).astype(bf16)
        hidden[rows, :] = low
        stream = stream + mm(low, down_ref[...]) + down_bias
        stream = jnp.where(live_rows(start, stream.shape, live), stream, 0.0).astype(bf16)
        three[rows, :] = stream
        prod[:, rows] = mm_nt(head_ref[...], stream)
        return carry

    loop(count, fore, 0)

    taps = 9 * latent_ch
    predicted = jnp.zeros((latent_ch, rows_n), f32) + head_bias_ref[...]
    for a in range(3):
        for b in range(3):
            tap = 3 * a + b
            predicted = predicted + tap_shift(
                prod[tap * latent_ch : (tap + 1) * latent_ch], a, b, freq_bins
            )
    pos = lax.broadcasted_iota(jnp.int32, predicted.shape, 1)
    errors = jnp.where(pos < live, predicted - noiT_ref[...], 0.0)
    small_ref[:, 0:128] = jnp.broadcast_to(
        jnp.sum(errors, axis=1, keepdims=True), (latent_ch, 128)
    )
    small_ref[:, 128:256] = jnp.broadcast_to(
        jnp.sum(errors * errors, axis=1, keepdims=True), (latent_ch, 128)
    )
    errors = errors.astype(bf16).astype(f32)
    for a in range(3):
        for b in range(3):
            tap = 3 * a + b
            prod[tap * latent_ch : (tap + 1) * latent_ch] = tap_shift(
                errors, 2 - a, 2 - b, freq_bins
            )
    prod[taps:] = jnp.zeros((prod.shape[0] - taps, rows_n), f32)
    gcols[...] = prod[...].T.astype(bf16)
    ghead_ref[...] = mm(prod[0:taps].astype(bf16), three[...])

    def back(i, carry):
        g_down, g_up, g_gain, g_shift, g_proj = carry
        start = pl.multiple_of(i * CHUNK, CHUNK)
        rows = pl.ds(start, CHUNK)
        grad = mm(gcols[rows, :], head_ref[...])
        grad = jnp.where(live_rows(start, grad.shape, live), grad, 0.0)
        low = grad.astype(bf16)
        three_t[:, rows] = low.T
        pre = mm_nt(low, down_ref[...]) * slope[rows, :]
        pre_low = pre.astype(bf16)
        gpre[rows, :] = pre_low
        dnormed = mm_nt(pre_low, wide_ref[:, 4 * channels :])
        hat = xhat[rows, :]
        dhat = dnormed * gain
        dstream = (dhat - row_mean(dhat) - hat * row_mean(dhat * hat)) * spread[rows, 0:1]
        two = grad + dstream
        two_grad_ref[rows, :] = two
        two_low = two.astype(bf16)
        glow[rows, :] = two_low
        do_ref[:, rows] = mm_nt(w_out, two_low).astype(bf16)
        return (
            g_down + col_sum(grad),
            g_up + col_sum(pre),
            g_gain + col_sum(dnormed * hat),
            g_shift + col_sum(dnormed),
            g_proj + col_sum(two),
        )

    blank = jnp.zeros((1, channels), f32)
    sums = loop(count, back, (blank, jnp.zeros((1, units), f32), blank, blank, blank))
    gvec_ref[...] = jnp.zeros(gvec_ref.shape, f32)
    for index, value in zip((11, 16, 9, 10, 8), sums):
        start, length = segs[index]
        gvec_ref[:, start : start + length] = value
    gproj_ref[...] = mm(mixed_ref[...].astype(bf16), glow[...]).astype(bf16)
    for part in range(units // channels):
        columns = slice(part * channels, (part + 1) * channels)
        gdown_ref[columns, :] = mm(three_t[...], hidden[:, columns]).T.astype(bf16)
        gup_ref[:, columns] = mm(normed_t[...], gpre[:, columns]).astype(bf16)


def hind_kernel(
    freq_bins,
    groups,
    len_ref,
    dq_ref,
    dk_ref,
    dv_ref,
    two_grad_ref,
    normed_ref,
    one_ref,
    act_two_ref,
    inner_ref,
    act_one_ref,
    zero_ref,
    colsT_ref,
    stat_ref,
    film_ref,
    conv_ref,
    wide_ref,
    time_ref,
    vec_ref,
    wave_ref,
    gqkv_ref,
    gconv_ref,
    gstem_ref,
    gvec_ref,
    factor_ref,
    buf,
    field,
    other,
    act_t,
):
    rows_n, channels = one_ref.shape
    embed = time_ref.shape[1]
    latent_ch = colsT_ref.shape[0] // 9
    count = rows_n // CHUNK
    live = len_ref[0] * freq_bins
    counted = (live * (channels // groups)).astype(f32)
    segs = offsets(channels, embed, FF, latent_ch)
    blank = jnp.zeros((1, channels), f32)
    gvec_ref[...] = jnp.zeros(gvec_ref.shape, f32)

    def seg(index):
        start, length = segs[index]
        return vec_ref[:, start : start + length]

    def put_vec(index, value):
        start, length = segs[index]
        gvec_ref[:, start : start + length] = value

    for part, ref in enumerate((dq_ref, dk_ref, dv_ref)):
        columns = slice(part * channels, (part + 1) * channels)
        gqkv_ref[:, columns] = mm(ref[...], normed_ref[...]).T.astype(bf16)

    gain_one = seg(6)
    clear_ends(buf, rows_n, freq_bins)

    def norm_part(i, carry):
        g_gain, g_shift, g_bias = carry
        start = pl.multiple_of(i * CHUNK, CHUNK)
        rows = pl.ds(start, CHUNK)
        dnormed_t = None
        for part, ref in enumerate((dq_ref, dk_ref, dv_ref)):
            term = mm(wide_ref[:, part * channels : (part + 1) * channels], ref[:, rows])
            dnormed_t = term if dnormed_t is None else dnormed_t + term
        dnormed = dnormed_t.T
        stream = one_ref[rows, :]
        gap = stream - row_mean(stream)
        scale = lax.rsqrt(row_mean(gap * gap) + norm_floor)
        hat = gap * scale
        dhat = dnormed * gain_one
        grad = two_grad_ref[rows, :] + scale * (
            dhat - row_mean(dhat) - hat * row_mean(dhat * hat)
        )
        field[rows, :] = grad
        put_shifted(buf, start, grad.astype(bf16).astype(f32), freq_bins)
        return (
            g_gain + col_sum(dnormed * hat),
            g_shift + col_sum(dnormed),
            g_bias + col_sum(grad),
        )

    sums = loop(count, norm_part, (blank, blank, blank))
    for index, value in zip((6, 7, 5), sums):
        put_vec(index, value)

    def weight_grad(which, act_ref):
        act_t[...] = act_ref[...].T
        for a in range(3):
            full = buf[freq_bins * (2 - a) : freq_bins * (2 - a) + rows_n, :]
            for b in range(3):
                shifted = full[:, (2 - b) * channels : (3 - b) * channels]
                first = (3 * a + b) * channels
                gconv_ref[which, first : first + channels, :] = mm(act_t[...], shifted).astype(
                    bf16
                )

    def input_grad(which, start):
        total = None
        for a in range(3):
            for b in range(3):
                first = (3 * (2 - a) + 2 - b) * channels
                part = mm_nt(
                    buf[
                        pl.ds(start + freq_bins * a, CHUNK),
                        b * channels : (b + 1) * channels,
                    ],
                    conv_ref[which, first : first + channels, :],
                )
                total = part if total is None else total + part
        return total

    def norm_back(which, read, center, scale, gain, shift, g_refs):
        def part(i, carry):
            g_gain, g_shift = carry
            start = pl.multiple_of(i * CHUNK, CHUNK)
            rows = pl.ds(start, CHUNK)
            hat = (read(start) - center) * scale
            slope = silu_slope(hat * gain + shift)
            grad = input_grad(which, start) * slope
            grad = jnp.where(live_rows(start, grad.shape, live), grad, 0.0)
            other[rows, :] = grad
            return (g_gain + col_sum(grad * hat), g_shift + col_sum(grad))

        g_gain, g_shift = loop(count, part, (blank, blank))
        put_vec(g_refs[0], g_gain)
        put_vec(g_refs[1], g_shift)
        mean_grad = group_total(g_shift * gain, groups) / counted
        mean_hat = group_total(g_gain * gain, groups) / counted

        def finish(start):
            hat = (read(start) - center) * scale
            grad = (other[pl.ds(start, CHUNK), :] * gain - mean_grad - hat * mean_hat) * scale
            return jnp.where(live_rows(start, grad.shape, live), grad, 0.0)

        return finish

    film = film_ref[0:1]
    lift = 1.0 + film[:, :channels]
    move = film[:, channels:]

    weight_grad(1, act_two_ref)
    finish = norm_back(
        1,
        lambda start: inner_ref[pl.ds(start, CHUNK), :] * lift + move,
        stat_ref[2:3],
        stat_ref[3:4],
        seg(3),
        seg(4),
        (3, 4),
    )

    def inner_part(i, carry):
        g_lift, g_move, g_bias = carry
        start = pl.multiple_of(i * CHUNK, CHUNK)
        moved = finish(start)
        grad = moved * lift
        put_shifted(buf, start, grad.astype(bf16).astype(f32), freq_bins)
        return (
            g_lift + col_sum(moved * inner_ref[pl.ds(start, CHUNK), :]),
            g_move + col_sum(moved),
            g_bias + col_sum(grad),
        )

    g_lift, g_move, g_bias = loop(count, inner_part, (blank, blank, blank))
    put_vec(2, g_bias)

    weight_grad(0, act_one_ref)
    finish_zero = norm_back(
        0,
        lambda start: zero_ref[pl.ds(start, CHUNK), :],
        stat_ref[0:1],
        stat_ref[1:2],
        seg(0),
        seg(1),
        (0, 1),
    )

    def zero_part(i, carry):
        g_stem, g_bias = carry
        start = pl.multiple_of(i * CHUNK, CHUNK)
        rows = pl.ds(start, CHUNK)
        grad = field[rows, :] + finish_zero(start)
        return (g_stem + mm(colsT_ref[:, rows], grad.astype(bf16)), g_bias + col_sum(grad))

    g_stem, g_bias = loop(
        count, zero_part, (jnp.zeros((colsT_ref.shape[0], channels), f32), blank)
    )
    gstem_ref[...] = g_stem
    put_vec(12, g_bias)

    pre_time = film_ref[1:2]
    embedding = film_ref[2:3]
    g_film = jnp.concatenate([g_lift, g_move], 1)
    g_embed = vec_mat(g_film, time_ref[2], True) * silu_slope(embedding)
    g_time = vec_mat(g_embed, time_ref[1], True) * silu_slope(pre_time)
    put_vec(13, g_time)
    put_vec(14, g_embed)
    put_vec(15, g_film)
    factor_ref[0:1] = wave_ref[...]
    factor_ref[1:2] = jax.nn.silu(pre_time)
    factor_ref[2:3] = jax.nn.silu(embedding)
    factor_ref[3:4] = g_time
    factor_ref[4:5] = g_embed
    factor_ref[5:6] = g_film
    factor_ref[6:8] = jnp.zeros((2, embed), f32)


def sized(shape, dtype=f32):
    return jax.ShapeDtypeStruct(shape, dtype)


VM = pl.BlockSpec(memory_space=pltpu.VMEM)
SM = pl.BlockSpec(memory_space=pltpu.SMEM)


def params(mib):
    return pltpu.CompilerParams(vmem_limit_bytes=mib * 2**20)


def run_fore(freq_bins, length, mix, lat, noi, stem_w, conv, wide_qkv, time_low, vec, wave, clap):
    rows_n, latent_ch = lat.shape
    channels = stem_w.shape[1]
    embed = time_low.shape[1]
    field = sized((rows_n, channels))
    field_low = sized((rows_n, channels), bf16)
    return pl.pallas_call(
        functools.partial(fore_kernel, freq_bins, GROUPS),
        in_specs=[SM, SM] + [VM] * 9,
        out_specs=[VM] * 11,
        out_shape=[
            field,
            field_low,
            field,
            field_low,
            field,
            field_low,
            sized((3 * channels, rows_n), bf16),
            sized((9 * latent_ch, rows_n), bf16),
            sized((latent_ch, rows_n)),
            sized((8, channels)),
            sized((8, embed)),
        ],
        scratch_shapes=[
            pltpu.VMEM((rows_n + 2 * freq_bins, 3 * channels), bf16),
            pltpu.VMEM((rows_n, 128), bf16),
            pltpu.VMEM((128, rows_n), f32),
        ],
        compiler_params=params(48),
        name="fore",
    )(length, mix, lat, noi, stem_w, conv, wide_qkv, time_low, vec, wave, clap)


def run_attend(freq_bins, length, qkv_t, key_block=256):
    triple, rows_n = qkv_t.shape
    channels = triple // 3
    dim = channels // HEADS
    return pl.pallas_call(
        functools.partial(attend_kernel, freq_bins, key_block),
        grid=(HEADS,),
        in_specs=[SM]
        + [pl.BlockSpec((dim, rows_n), lambda h, t=t: (t * HEADS + h, 0)) for t in range(3)],
        out_specs=[
            pl.BlockSpec((dim, rows_n), lambda h: (h, 0)),
            pl.BlockSpec((1, 1, rows_n), lambda h: (h, 0, 0)),
        ],
        out_shape=[sized((channels, rows_n)), sized((HEADS, 1, rows_n))],
        scratch_shapes=[
            pltpu.VMEM((rows_n, 128), bf16),
            pltpu.VMEM((128, rows_n), bf16),
            pltpu.VMEM((dim + 16, rows_n), bf16),
        ],
        compiler_params=params(48),
        name="attend",
    )(length, qkv_t, qkv_t, qkv_t)


def run_attend_back(freq_bins, length, qkv_t, lse, mixed_t, grad_t, key_block=512):
    triple, rows_n = qkv_t.shape
    channels = triple // 3
    dim = channels // HEADS
    whole = pl.BlockSpec((dim, rows_n), lambda h, j: (h, 0))
    block = pl.BlockSpec((dim, key_block), lambda h, j: (h, j))
    return pl.pallas_call(
        functools.partial(attend_back_kernel, freq_bins, key_block),
        grid=(HEADS, rows_n // key_block),
        in_specs=[SM]
        + [pl.BlockSpec((dim, rows_n), lambda h, j, t=t: (t * HEADS + h, 0)) for t in range(3)]
        + [pl.BlockSpec((1, 1, rows_n), lambda h, j: (h, 0, 0)), whole, whole],
        out_specs=[whole, block, block],
        out_shape=[sized((channels, rows_n), bf16)] * 3,
        scratch_shapes=[
            pltpu.VMEM((rows_n, 128), bf16),
            pltpu.VMEM((128, rows_n), bf16),
            pltpu.VMEM((rows_n, 128), bf16),
            pltpu.VMEM((128, rows_n), bf16),
            pltpu.VMEM((dim, rows_n), f32),
        ],
        compiler_params=params(48),
        name="attend_back",
    )(length, qkv_t, qkv_t, qkv_t, lse, mixed_t, grad_t)


def run_middle(freq_bins, length, mixed_t, one, wide, down, vec, head_t, head_bias, noi_t):
    rows_n, channels = one.shape
    units = down.shape[0]
    latent_ch = noi_t.shape[0]
    return pl.pallas_call(
        functools.partial(middle_kernel, freq_bins),
        in_specs=[SM] + [VM] * 8,
        out_specs=[VM] * 8,
        out_shape=[
            sized((rows_n, channels)),
            sized((channels, rows_n), bf16),
            sized((units, channels), bf16),
            sized((channels, units), bf16),
            sized((channels, channels), bf16),
            sized((9 * latent_ch, channels)),
            sized(vec.shape),
            sized((latent_ch, 256)),
        ],
        scratch_shapes=[
            pltpu.VMEM((rows_n, units), bf16),
            pltpu.VMEM((rows_n, units), f32),
            pltpu.VMEM((rows_n, channels), f32),
            pltpu.VMEM((rows_n, 128), f32),
            pltpu.VMEM((rows_n, channels), bf16),
            pltpu.VMEM((128, rows_n), f32),
            pltpu.VMEM((rows_n, 128), bf16),
            pltpu.VMEM((channels, rows_n), bf16),
            pltpu.VMEM((channels, rows_n), bf16),
            pltpu.VMEM((rows_n, units), bf16),
            pltpu.VMEM((rows_n, channels), bf16),
        ],
        compiler_params=params(56),
        name="middle",
    )(length, mixed_t, one, wide, down, vec, head_t, head_bias, noi_t)


def run_hind(freq_bins, length, *arrays):
    one = arrays[5]
    rows_n, channels = one.shape
    cols_t = arrays[10]
    vec = arrays[16]
    embed = arrays[15].shape[1]
    return pl.pallas_call(
        functools.partial(hind_kernel, freq_bins, GROUPS),
        in_specs=[SM] + [VM] * len(arrays),
        out_specs=[VM] * 5,
        out_shape=[
            sized((channels, 3 * channels), bf16),
            sized((2, 9 * channels, channels), bf16),
            sized((cols_t.shape[0], channels)),
            sized(vec.shape),
            sized((8, embed)),
        ],
        scratch_shapes=[
            pltpu.VMEM((rows_n + 2 * freq_bins, 3 * channels), bf16),
            pltpu.VMEM((rows_n, channels), f32),
            pltpu.VMEM((rows_n, channels), f32),
            pltpu.VMEM((channels, rows_n), bf16),
        ],
        compiler_params=params(56),
        name="hind",
    )(length, *arrays)


def noise_mix(step_value):
    phase = (step_value.astype(f32) / 1000.0 + 0.008) / 1.008 * (math.pi / 2)
    keep_part = jnp.cos(phase) ** 2
    return jnp.stack([jnp.sqrt(keep_part), jnp.sqrt(1.0 - keep_part)])


def adam_step(weight, moment_one, moment_two, gradient, decay_on, fix_one, fix_two):
    first_new = 0.9 * moment_one + 0.1 * gradient
    second_new = 0.999 * moment_two + 0.001 * gradient * gradient
    moved = first_new / fix_one / (jnp.sqrt(second_new / fix_two) + adam_floor)
    return (weight - adam_rate * (moved + decay_on * weight), first_new, second_new)


def local(
    latents,
    noises,
    clap_embed,
    timesteps,
    lengths,
    step_count,
    stem_w,
    head_w,
    time_w,
    vector,
    conv_w,
    wide_w,
    down_w,
    roots_small,
    root_wide,
    roots_large,
    stem_moment,
    stem_square,
    head_moment,
    head_square,
    time_moment,
    time_square,
    vector_moment,
    vector_square,
    conv_moment,
    conv_square,
    wide_moment,
    down_moment,
):
    frames_n, freq_bins, latent_ch = (latents.shape[1], latents.shape[2], latents.shape[3])
    channels = stem_w.shape[1]
    embed = time_w.shape[2]
    rows_n = frames_n * freq_bins
    both = ("dp", "fsdp")
    here = lax.axis_index("fsdp")

    def gather(value, dim):
        return lax.all_gather(value.astype(bf16), "fsdp", axis=dim, tiled=True)

    conv_full = gather(conv_w, 1)
    time_full = gather(time_w, 1)
    wide_full = gather(wide_w, 0)
    down_full = gather(down_w, 0)
    wide_moment_full = gather(wide_moment, 0)
    down_moment_full = gather(down_moment, 0)

    half_width = embed // 2
    frequency = jnp.exp(-math.log(10000.0) * jnp.arange(half_width).astype(f32) / half_width)
    angles = timesteps[0].astype(f32) * frequency
    wave = jnp.concatenate([jnp.cos(angles), jnp.sin(angles)])[None]
    vec = vector[None]
    head_t = jnp.pad(
        head_w.reshape(9, channels, latent_ch).transpose(0, 2, 1).reshape(-1, channels),
        ((0, 128 - 9 * latent_ch), (0, 0)),
    ).astype(bf16)
    head_bias = vector[-latent_ch:][:, None]

    (
        zero,
        act_one,
        inner,
        act_two,
        one,
        normed,
        qkv_t,
        cols_t,
        noi_t,
        stat,
        film,
    ) = run_fore(
        freq_bins,
        lengths,
        noise_mix(timesteps[0]),
        latents.reshape(rows_n, latent_ch),
        noises.reshape(rows_n, latent_ch),
        stem_w,
        conv_full,
        wide_full[:, : 3 * channels],
        time_full,
        vec,
        wave,
        clap_embed,
    )
    mixed_t, lse = run_attend(freq_bins, lengths, qkv_t)
    two_grad, do_t, gdown, gup, gproj, ghead_t, gvec_mid, small = run_middle(
        freq_bins, lengths, mixed_t, one, wide_full, down_full, vec, head_t, head_bias, noi_t
    )
    gdown, gup, gproj = lax.psum((gdown, gup, gproj), both)
    dq, dk, dv = run_attend_back(freq_bins, lengths, qkv_t, lse, mixed_t, do_t)
    gqkv, gconv, gstem, gvec_hind, factors = run_hind(
        freq_bins,
        lengths,
        dq,
        dk,
        dv,
        two_grad,
        normed,
        one,
        act_two,
        inner,
        act_one,
        zero,
        cols_t,
        stat,
        film,
        conv_full,
        wide_full,
        time_full,
        vec,
        wave,
    )

    conv_shard = lax.psum_scatter(gconv, "fsdp", scatter_dimension=1, tiled=True)
    conv_shard = lax.psum(conv_shard, "dp").astype(f32)
    gqkv = lax.psum(gqkv, both)
    gvec_head = jnp.pad(small[:, 0], (vector.shape[0] - latent_ch, 0))
    gvec = gvec_mid[0] + gvec_hind[0] + gvec_head
    loss_local = jnp.sum(small[:, 128])
    live_local = lengths[0].astype(f32) * freq_bins
    loss_sum, live_count, gstem, ghead_t, gvec = lax.psum(
        (loss_local, live_local, gstem, ghead_t, gvec), both
    )
    ghead = ghead_t.reshape(9, latent_ch, channels).transpose(0, 2, 1).reshape(-1, latent_ch)
    everyone = lax.all_gather(factors, both, axis=0)
    rows_here = time_w.shape[1]
    sides = lax.dynamic_slice_in_dim(everyone[:, 0:3], here * rows_here, rows_here, 2)
    time_shard = jnp.einsum("niw,niv->iwv", sides, everyone[:, 3:6], precision=highest)

    def squares(value):
        value = value.astype(f32)
        return jnp.sum(value * value)

    shard_total = lax.psum(squares(conv_shard) + squares(time_shard), "fsdp")
    total = (
        shard_total
        + squares(gstem)
        + squares(ghead)
        + squares(gvec)
        + squares(gdown)
        + squares(gup)
        + squares(gproj)
        + squares(gqkv)
    )
    unit = 2.0 / (latent_ch * live_count)
    loss_value = loss_sum / (latent_ch * live_count)
    grad_norm = unit * jnp.sqrt(total)
    factor = jnp.minimum(1.0, clip_limit / grad_norm) * unit
    step_value = step_count[0].astype(f32)
    fix_one = 1.0 - jnp.power(0.9, step_value)
    fix_two = 1.0 - jnp.power(0.999, step_value)
    vector_clipped = factor * gvec

    def adam(weight, first, second, grad, decay_on):
        return adam_step(weight, first, second, grad, decay_on, fix_one, fix_two)

    stem_out = adam(stem_w, stem_moment, stem_square, factor * gstem, decay_rate)
    head_out = adam(head_w, head_moment, head_square, factor * ghead, decay_rate)
    time_out = adam(time_w, time_moment, time_square, factor * time_shard, decay_rate)
    vector_out = adam(vector, vector_moment, vector_square, vector_clipped, 0.0)
    conv_out = adam(conv_w, conv_moment, conv_square, factor * conv_shard, decay_rate)

    wide_rows = wide_w.shape[0]
    down_rows = down_w.shape[0]
    gwide = jnp.concatenate([gqkv, gproj, gup], 1)
    wide_mine = lax.dynamic_slice_in_dim(gwide, here * wide_rows, wide_rows, 0)
    down_mine = lax.dynamic_slice_in_dim(gdown, here * down_rows, down_rows, 0)
    wide_moment_new = 0.9 * wide_moment + factor * wide_mine.astype(f32)
    down_moment_new = 0.9 * down_moment + factor * down_mine.astype(f32)

    def direction(left_root, moment_full, grad_full, right_root, rows):
        left = lax.dynamic_slice_in_dim(left_root, here * rows, rows, 0).astype(bf16)
        moment_now = 0.9 * moment_full.astype(f32) + factor * grad_full.astype(f32)
        left_done = mm(left, moment_now.astype(bf16))
        return mm(left_done.astype(bf16), right_root.astype(bf16))

    bounds = (0, 3 * channels, 4 * channels, 4 * channels + FF)
    rights = (root_wide, roots_small[3], roots_large[0])
    directions = []
    for index in range(3):
        columns = slice(bounds[index], bounds[index + 1])
        directions.append(
            direction(
                roots_small[index],
                wide_moment_full[:, columns],
                gwide[:, columns],
                rights[index],
                wide_rows,
            )
        )
    wide_new = wide_w * (1.0 - shampoo_rate * decay_rate) - shampoo_rate * jnp.concatenate(
        directions, 1
    )
    down_direction = direction(
        roots_large[1], down_moment_full, gdown, roots_small[4], down_rows
    )
    down_new = down_w * (1.0 - shampoo_rate * decay_rate) - shampoo_rate * down_direction
    return (
        loss_value,
        grad_norm,
        stem_out[0],
        stem_out[1],
        stem_out[2],
        head_out[0],
        head_out[1],
        head_out[2],
        time_out[0],
        time_out[1],
        time_out[2],
        vector_clipped,
        vector_out[1],
        vector_out[2],
        conv_out[0],
        conv_out[1],
        conv_out[2],
        wide_new,
        wide_moment_new,
        down_new,
        down_moment_new,
    )


def solution(mesh):
    in_specs = (
        P(("dp", "fsdp"), None, None, None),
        P(("dp", "fsdp"), None, None, None),
        P(("dp", "fsdp"), None),
        P(("dp", "fsdp")),
        P(("dp", "fsdp")),
        P(),
        P(),
        P(),
        P(None, "fsdp", None),
        P(),
        P(None, "fsdp", None),
        P("fsdp", None),
        P("fsdp", None),
        P(),
        P(),
        P(),
        P(),
        P(),
        P(),
        P(),
        P(None, "fsdp", None),
        P(None, "fsdp", None),
        P(),
        P(),
        P(None, "fsdp", None),
        P(None, "fsdp", None),
        P("fsdp", None),
        P("fsdp", None),
    )
    out_specs = (
        P(),
        P(),
        P(),
        P(),
        P(),
        P(),
        P(),
        P(),
        P(None, "fsdp", None),
        P(None, "fsdp", None),
        P(None, "fsdp", None),
        P(),
        P(),
        P(),
        P(None, "fsdp", None),
        P(None, "fsdp", None),
        P(None, "fsdp", None),
        P("fsdp", None),
        P("fsdp", None),
        P("fsdp", None),
        P("fsdp", None),
    )
    return jax.shard_map(local, mesh=mesh, in_specs=in_specs, out_specs=out_specs, check_vma=False)
```

time: 1500 us -> 745 us (0.50); the launches traced: 1480 us -> 744 us
  matrix products: 542 us -> 10.2 us
  local copies, waits for them, and re-layouts: 274 us -> 21.1 us
  other arithmetic: 258 us -> 29.1 us
  Pallas kernels: 0 us -> 216 us
  waiting for transfers between devices: 249 us -> 305 us
  blocking collectives: 117 us -> 135 us
    dot_general x64 -> x5, matrix products: 542 us -> 10.2 us  [the longest x4 9.02 us: mm(): return jnp.dot(left_op, right_op, preferred_element_type=f32)]
    pallas_call x0 -> x5, Pallas kernels: none -> 216 us  [the longest x1 95.5 us: run_attend_back(): pl.pallas_call(functools.partial(attend_back_kernel, freq_bins, key_block...]
    convert_element_type x18 -> x4, other arithmetic: 126 us -> 5.18 us  [gather(): return lax.all_gather(value.astype(bf16), 'fsdp', axis=dim, tiled=True)]
    reduce_sum x41 -> x8, other arithmetic: 101 us -> 12.7 us  [squares(): return jnp.sum(value * value)]
    psum x2 -> x3, waiting for transfers between devices: 135 us -> 205 us  [the longest x1 139 us: local(): gdown, gup, gproj = lax.psum((gdown, gup, gproj), both)]
    unnamed x363 -> x104, local copies, waits for them, and re-layouts: 79.4 us -> 13.9 us
    slice x8 -> x3, local copies, waits for them, and re-layouts: 65.6 us -> 1.86 us  [the longest x1 1.02 us: local(): wide_full[:, :3 * channels]]
    all_gather x3 -> x4, waiting for transfers between devices: 0.03 us -> 61.9 us  [gather(): return lax.all_gather(value.astype(bf16), 'fsdp', axis=dim, tiled=True)]
  transfers between devices with their start and end apart: 13 -> 8, of which waited for: 8 -> 7; matrix products, arithmetic and copies ran while one was open for 45% -> 4% of each run, Pallas kernels for 0% -> 0%
where the time goes in v1:
time: 745 us; the launch traced here: 744 us
  waiting for transfers between devices  305 us (41%)
  Pallas kernels  216 us (29%)
  blocking collectives  135 us (18%)
  other arithmetic  29.1 us (4%)
  between operations  26.9 us (4%)
  local copies, waits for them, and re-layouts  21.1 us (3%)
  matrix products  10.2 us (1%)
    psum x1, waiting for transfers between devices, local(): gdown, gup, gproj = lax.psum((gdown, gup, gproj), both)  139 us
    pallas_call x1, Pallas kernels, run_attend_back(): pl.pallas_call(functools.partial(attend_back_kernel, freq_bins, key_block...  95.5 us
    all_gather x4, waiting for transfers between devices, gather(): return lax.all_gather(value.astype(bf16), 'fsdp', axis=dim, tiled=True)  61.9 us
    all_gather x1, blocking collectives, local(): everyone = lax.all_gather(factors, both, axis=0)  41.8 us
    psum x1, blocking collectives, local(): lax.psum((loss_local, live_local, gstem, ghead_t, gvec), both)  40.8 us
    psum x1, waiting for transfers between devices, local(): conv_shard = lax.psum(conv_shard, 'dp').astype(f32)  39.4 us
    reduce_scatter x1, waiting for transfers between devices, local(): lax.psum_scatter(gconv, 'fsdp', scatter_dimension=1, tiled=True)  37.6 us
    pallas_call x1, Pallas kernels, run_attend(): pl.pallas_call(functools.partial(attend_kernel, freq_bins, key_block), gr...  36.9 us
  transfers between devices with their start and end apart: 8, of which 7 were waited for; matrix products, arithmetic and copies ran while one was open for 4% of the time, Pallas kernels for 0%

profile of v1, /device:TPU:0, one launch (start us, length us, event | category | flops | bytes accessed | tf_op | source)
XLA Modules:
  0.0 743.7 jit_solution(13268943153497465861)
XLA Ops:
  7.3 1.7 convert_element_type.144
  9.0 1.7 convert_element_type.145
  10.8 1.8 convert_element_type.143
  16.6 19.3 %all_gather.27.down_ref = bf16[1024,256]{1,0:T(8,128)(2,1)} all-gather(bf16[128,256]{1,0:T(8,128)(2,1)S(1)} %convert_element_type.147), channel_id=1, replica_groups=mesh['dp'=4,'fsdp'=8] {'fsdp'}, dimensions={0}, use_global_device_ids=true | all-gather | bytes 589824 | tf_op jit(solution)/shard_map/all_gather | solution.py:978
  36.0 2.2 all-gather.8.cloned.1.call-done.wide_ref
  38.2 1.0 slice.67.wide_ref
  39.2 26.3 %all-gather.10.cloned.1.call-done.time_ref = bf16[3,512,512]{2,1,0:T(8,128)(2,1)} async-done(((bf16[3,64,512]{2,1,0:T(8,128)(2,1)}), bf16[3,512,512]{2,1,0:T(8,128)(2,1)}) %all-gather.10.cloned.1.call-update) | async-done | bytes 1572880 | tf_op jit(solution)/shard_map/all_gather | solution.py:978
  65.5 33.4 %all-gather.6.cloned.1.call-done.conv_ref = bf16[2,2304,256]{2,1,0:T(8,128)(2,1)} async-done(((bf16[2,288,256]{2,1,0:T(8,128)(2,1)}), bf16[2,2304,256]{2,1,0:T(8,128)(2,1)}) %all-gather.6.cloned.1.call-update) | async-done | bytes 2359312 | tf_op jit(solution)/shard_map/all_gather | solution.py:978
  98.9 25.8 %fore.1 = (f32[2048,256]{1,0:T(8,128)}, bf16[2048,256]{1,0:T(8,128)(2,1)S(1)}, f32[2048,256]{1,0:T(8,128)}, bf16[2048,256]{1,0:T(8,128)(2,1)S(1)}, f32[2048,256]...) custom-call(s32[1]{0:T(128)S(6)} %copy.78.len_ref, ...), custom_call_target="tpu_custom_call" | custom-call | tf_op jit(solution)/shard_map/fore/pallas_call | solution.py:786
  124.6 1.0 copy-done.2
  125.6 1.0 copy-done.3
  126.6 1.0 copy-done.4
  130.1 1.9 copy-done
  132.0 36.9 %attend.1 = (f32[256,2048]{1,0:T(8,128)S(1)}, f32[8,1,2048]{2,1,0:T(1,128)S(1)}) custom-call(s32[1]{0:T(128)S(6)} %copy.78.len_ref, bf16[768,2048]{1,0:T(8,128)(2,1)S(1)} %copy-done, bf16[768,2048]{1,0:T(8,128)(2,1)S(1)} %copy-done, bf16[768,2048]{1,0:T(8,128)(2,1)S(1)} %copy-done), custom_call_target="tpu_custom_call" | custom-call | tf_op jit(solution)/shard_map/attend/pallas_call | solution.py:817
  168.9 1.3 copy-done.1
  170.2 24.8 %middle.1 = (f32[2048,256]{1,0:T(8,128)}, bf16[256,2048]{1,0:T(8,128)(2,1)}, bf16[1024,256]{1,0:T(8,128)(2,1)}, bf16[256,1024]{1,0:T(8,128)(2,1)}, bf16[256,256]...) custom-call(s32[1]{0:T(128)S(6)} %copy.78.len_ref, f32[256,2048]{1,0:T(8,128)} %copy-done.1, ...), custom_call_target="tpu_custom_call" | custom-call | tf_op jit(solution)/shard_map/middle/pallas_call | solution.py:867
  195.0 1.2 copy-done.8
  196.2 95.5 %attend_back.1 = (bf16[256,2048]{1,0:T(8,128)(2,1)S(1)}, bf16[256,2048]{1,0:T(8,128)(2,1)S(1)}, bf16[256,2048]{1,0:T(8,128)(2,1)S(1)}) custom-call(s32[1]{0:T(128)S(6)} %copy.78.len_ref, bf16[768,2048]{1,0:T(8,128)(2,1)} %get-tuple-element.50.q_ref.k_ref.v_ref, bf16[768,2048]{1,0:T(8,128)(2,1)} %get-tuple-element.50.q_ref.k_ref.v_ref, ...), custom_call_target="tpu_custom_call" | custom-call | tf_op jit(solution)/shard_map/attend_back/pallas_call | solution.py:843
  291.7 1.0 copy-done.5
  292.7 1.0 copy-done.6
  293.7 1.0 copy-done.7
  294.6 32.7 %hind.1 = (bf16[256,768]{1,0:T(8,128)(2,1)}, bf16[2,2304,256]{2,1,0:T(8,128)(2,1)}, f32[72,256]{1,0:T(8,128)}, f32[1,5896]{1,0:T(1,128)}, f32[8,512]{1,0:T(8,128)}) custom-call(s32[1]{0:T(128)S(6)} %copy.78.len_ref, bf16[256,2048]{1,0:T(8,128)(2,1)} %copy-done.5, bf16[256,2048]{1,0:T(8,128)(2,1)} %copy-done.6, bf16[256,2048]{1,0:T(8,128)(2,1)} %copy-done.7, ...), custom_call_target="tpu_custom_call" | custom-call | tf_op jit(solution)/shard_map/hind/pallas_call | solution.py:905
  328.7 0.9 convert.15
  329.7 3.9 slice.65
  333.6 0.8 fusion.98
  335.1 40.8 %all-reduce.2 = (f32[]{:T(128)}, f32[]{:T(128)}, f32[5896]{0:T(1024)S(1)}) all-reduce(f32[]{:T(128)} %get-tuple-element.80, f32[]{:T(128)} %bitcast.10, f32[5896]{0:T(1024)S(1)} %pad_add_fusion), channel_id=1, replica_groups=mesh['dp'=4,'fsdp'=8] {'dp','fsdp'}, use_global_device_ids=true, to_apply=%region_1.2 | all-reduce | flops 5898 | bytes 47184 | tf_op jit(solution)/shard_map/psum | solution.py:1060
  377.9 41.8 %all-gather = f32[256,512]{1,0:T(8,128)S(1)} all-gather(f32[8,512]{1,0:T(8,128)S(1)} %copy-done.49), channel_id=2, replica_groups=mesh['dp'=4,'fsdp'=8] {'dp','fsdp'}, dimensions={0}, use_global_device_ids=true | all-gather | bytes 540672 | tf_op jit(solution)/shard_map/all_gather | solution.py:1064
  420.3 1.2 multiply_reduce_fusion
  421.5 26.4 %all-reduce.11.cloned.1.call-done = (f32[72,256]{1,0:T(8,128)}, f32[72,256]{1,0:T(8,128)}) async-done(((f32[72,256]{1,0:T(8,128)}, f32[72,256]{1,0:T(8,128)}), (f32[72,256]{1,0:T(8,128)}, f32[72,256]{1,0:T(8,128)})) %all-reduce.11.cloned.1.call-update) | async-done | bytes 147472 | tf_op jit(solution)/shard_map/psum | solution.py:1060
  447.9 1.5 multiply_reduce_fusion.2
  449.5 1.5 multiply_reduce_fusion.1
  451.0 37.6 %reduce-scatter.2.cloned.1.call-done = bf16[2,288,256]{2,1,0:T(8,128)(2,1)} async-done(((bf16[2,2304,256]{2,1,0:T(8,128)(2,1)}), bf16[2,288,256]{2,1,0:T(8,128)(2,1)}) %reduce-scatter.2.cloned.1.call-update) | async-done | bytes 294928 | tf_op jit(solution)/shard_map/reduce_scatter | solution.py:1053
  488.6 138.9 %all-reduce.13.cloned.1.call-done = (bf16[1024,256]{1,0:T(8,128)(2,1)}, bf16[256,1024]{1,0:T(8,128)(2,1)}, bf16[256,256]{1,0:T(8,128)(2,1)}, bf16[256,768]{1,0:T(8,128)(2,1)}) async-done(((bf16[1024,256]{1,0:T(8,128)(2,1)}, bf16[256,1024]{1,0:T(8,128)(2,1)}, bf16[256,256]{1,0:T(8,128)(2,1)}, bf16[256,768]{1,0:T(8,128)(2,1)}), (bf16[1024,256]{1,0:T(8,128)(2,1)}, bf16[256,1024]{1,0:T(8,128)(2,1)}, ...) | async-done | bytes 1572880 | tf_op jit(solution)/shard_map/psum | solution.py:1028
  627.5 1.9 fusion.13
  629.4 1.9 fusion.7
  631.3 2.0 fusion.10
  633.3 39.4 %all-reduce.9.cloned.1.call-done = bf16[2,288,256]{2,1,0:T(8,128)(2,1)} async-done(((bf16[2,288,256]{2,1,0:T(8,128)(2,1)}), bf16[2,288,256]{2,1,0:T(8,128)(2,1)}) %all-reduce.9.cloned.1.call-update) | async-done | bytes 294928 | tf_op jit(solution)/shard_map/psum | solution.py:1054
  672.7 1.7 fusion.18
  675.7 1.6 fusion.43
  677.3 16.4 %psum.80 = f32[]{:T(128)} all-reduce(f32[]{:T(128)S(6)} %add.163), channel_id=1, replica_groups=mesh['dp'=4,'fsdp'=8] {'fsdp'}, use_global_device_ids=true, to_apply=%region_7.8 | all-reduce | flops 1 | bytes 8 | tf_op jit(solution)/shard_map/psum | solution.py:1073
  700.3 0.8 multiply_add_fusion.1
  701.8 16.9 %all_gather.31 = bf16[1024,256]{1,0:T(8,128)(2,1)} all-gather(bf16[128,256]{1,0:T(8,128)(2,1)S(1)} %get-tuple-element.112), channel_id=1, replica_groups=mesh['dp'=4,'fsdp'=8] {'fsdp'}, dimensions={0}, use_global_device_ids=true | all-gather | bytes 589824 | tf_op jit(solution)/shard_map/all_gather | solution.py:978
  720.1 2.4 fusion.5
  722.5 2.4 multiply_subtract_fusion.1
  725.0 1.5 multiply_subtract_fusion
  727.2 3.8 fusion.1
  731.0 1.3 fusion.6
  732.3 1.5 fusion.3
  (134 shorter events, 12.5 us)
Async XLA Ops:
  7.2 7.0 copy-start.42
  7.2 7.4 copy-start.43
  7.2 7.8 %copy-start.44 = (f32[5896]{0:T(1024)S(1)}, f32[5896]{0:T(1024)}, u32[]{:S(2)}) copy-start(f32[5896]{0:T(1024)} %param.37) | copy-start | bytes 70756
  7.2 7.9 %copy-start.36 = (f32[128,256]{1,0:T(8,128)S(1)}, f32[128,256]{1,0:T(8,128)}, u32[]{:S(2)}) copy-start(f32[128,256]{1,0:T(8,128)} %param.40) | copy-start | bytes 393220
  7.2 7.9 %copy-start.32 = (f32[2304,8]{0,1:T(8,128)S(1)}, f32[2304,8]{0,1:T(8,128)}, u32[]{:S(2)}) copy-start(f32[2304,8]{0,1:T(8,128)} %param.35) | copy-start | bytes 221188
  7.2 30.9 %all-gather.8.cloned.1.call-start = ((), (), s32[]{:S(2)}) async-start(), calls=%async_computation.2 | async-start | bytes 1179648 | tf_op jit(solution)/shard_map/all_gather | solution.py:978
  9.0 56.5 %all-gather.10.cloned.1.call-start = ((), (), s32[]{:S(2)}) async-start(), calls=%async_computation.3 | async-start | bytes 1769472 | tf_op jit(solution)/shard_map/all_gather | solution.py:978
  10.8 88.1 %copy-start.10 = (f32[72,256]{1,0:T(8,128)S(1)}, f32[72,256]{1,0:T(8,128)}, u32[]{:S(2)}) copy-start(f32[72,256]{1,0:T(8,128)} %stem_ref.1) | copy-start | bytes 221188
  10.8 88.1 %copy-start.16 = (f32[1,512]{1,0:T(1,128)S(1)}, f32[1,512]{1,0:T(1,128)}, u32[]{:S(2)}) copy-start(f32[1,512]{1,0:T(1,128)} %clap_ref.1) | copy-start | bytes 6148
  10.8 88.1 %all-gather.6.cloned.1.call-start = ((), (), s32[]{:S(2)}) async-start(), calls=%async_computation.1 | async-start | bytes 2654208 | tf_op jit(solution)/shard_map/all_gather | solution.py:978
  12.7 435.2 %all-reduce.11.cloned.1.call-start = ((), (), s32[]{:S(2)}) async-start(), calls=%async_computation.7 | async-start | bytes 294912 | tf_op jit(solution)/shard_map/psum | solution.py:1060
  15.1 109.5 %copy-start.9 = (f32[1,5896]{1,0:T(1,128)}, f32[1,5896]{1,0:T(1,128)S(1)}, u32[]{:S(2)}) copy-start(f32[1,5896]{1,0:T(1,128)S(1)} %broadcast_in_dim.9.vec_ref) | copy-start | bytes 70756
  16.6 108.0 %copy-start.13 = (f32[512]{0:T(512)}, f32[512]{0:T(512)S(1)}, u32[]{:S(2)}) copy-start(f32[512]{0:T(512)S(1)} %pad_maximum_fusion) | copy-start | bytes 6148
  130.1 1.9 copy-start
  168.9 1.3 copy-start.1
  327.3 1.4 copy-start.21
  327.3 161.2 %reduce-scatter.2.cloned.1.call-start = ((), (), s32[]{:S(2)}) async-start(), calls=%async_computation.4 | async-start | bytes 2654208 | tf_op jit(solution)/shard_map/reduce_scatter | solution.py:1053
  327.9 299.5 %all-reduce.13.cloned.1.call-start = ((), (), s32[]{:S(2)}) async-start(), calls=%async_computation.8 | async-start | bytes 3145728 | tf_op jit(solution)/shard_map/psum | solution.py:1028
  329.7 4.7 copy-start.50
  329.7 5.3 copy-start.47
  329.7 5.3 copy-start.48
  329.7 48.2 %copy-start.49 = (f32[8,512]{1,0:T(8,128)S(1)}, f32[8,512]{1,0:T(8,128)}, u32[]{:S(2)}) copy-start(f32[8,512]{1,0:T(8,128)} %get-tuple-element.70) | copy-start | bytes 49156
  419.8 253.0 %all-reduce.9.cloned.1.call-start = ((), (), s32[]{:S(2)}) async-start(), calls=%async_computation.5 | async-start | bytes 589824 | tf_op jit(solution)/shard_map/psum | solution.py:1054
  420.1 279.6 %copy-start.45 = (f32[5896]{0:T(1024)S(1)}, f32[5896]{0:T(1024)}, u32[]{:S(2)}) copy-start(f32[5896]{0:T(1024)} %param.51) | copy-start | bytes 70756
  420.1 280.2 %copy-start.34 = (f32[32,2048]{1,0:T(8,128)S(1)}, f32[32,2048]{1,0:T(8,128)}, u32[]{:S(2)}) copy-start(f32[32,2048]{1,0:T(8,128)} %param.54) | copy-start | bytes 786436
  447.9 251.1 %copy-start.31 = (f32[72,256]{1,0:T(8,128)S(1)}, f32[72,256]{1,0:T(8,128)}, u32[]{:S(2)}) copy-start(f32[72,256]{1,0:T(8,128)} %get-tuple-element.85) | copy-start | bytes 221188
  488.5 212.6 %copy-start.35 = (f32[128,256]{1,0:T(8,128)S(1)}, f32[128,256]{1,0:T(8,128)}, u32[]{:S(2)}) copy-start(f32[128,256]{1,0:T(8,128)} %param.55) | copy-start | bytes 393220
  488.5 238.7 %all-gather.12.cloned.1.call-start = ((), (), s32[]{:S(2)}) async-start(), calls=%async_computation.6 | async-start | bytes 1179648 | tf_op jit(solution)/shard_map/all_gather | solution.py:978
  627.5 72.8 %copy-start.17 = (bf16[256,1024]{1,0:T(8,128)(2,1)S(1)}, bf16[256,1024]{1,0:T(8,128)(2,1)}, u32[]{:S(2)}) copy-start(bf16[256,1024]{1,0:T(8,128)(2,1)} %get-tuple-element.87) | copy-start | bytes 1572868
  627.5 72.8 %copy-start.18 = (bf16[256,768]{1,0:T(8,128)(2,1)S(1)}, bf16[256,768]{1,0:T(8,128)(2,1)}, u32[]{:S(2)}) copy-start(bf16[256,768]{1,0:T(8,128)(2,1)} %get-tuple-element.89) | copy-start | bytes 1179652
  627.5 72.8 %copy-start.28 = (bf16[256,256]{1,0:T(8,128)(2,1)S(1)}, bf16[256,256]{1,0:T(8,128)(2,1)}, u32[]{:S(2)}) copy-start(bf16[256,256]{1,0:T(8,128)(2,1)} %get-tuple-element.88) | copy-start | bytes 393220
  627.5 73.7 %copy-start.25 = (bf16[1024,256]{1,0:T(8,128)(2,1)S(1)}, bf16[1024,256]{1,0:T(8,128)(2,1)}, u32[]{:S(2)}) copy-start(bf16[1024,256]{1,0:T(8,128)(2,1)} %get-tuple-element.86) | copy-start | bytes 1572868
  631.3 87.4 %copy-start.46 = (f32[5896]{0:T(1024)S(1)}, f32[5896]{0:T(1024)}, u32[]{:S(2)}) copy-start(f32[5896]{0:T(1024)} %param.50) | copy-start | bytes 70756
  631.3 88.0 %copy-start.30 = (f32[72,256]{1,0:T(8,128)S(1)}, f32[72,256]{1,0:T(8,128)}, u32[]{:S(2)}) copy-start(f32[72,256]{1,0:T(8,128)} %get-tuple-element.84) | copy-start | bytes 221188
  631.3 88.0 %copy-start.38 = (f32[72,256]{1,0:T(8,128)S(1)}, f32[72,256]{1,0:T(8,128)}, u32[]{:S(2)}) copy-start(f32[72,256]{1,0:T(8,128)} %param.45) | copy-start | bytes 221188
  631.3 88.0 %copy-start.39 = (f32[72,256]{1,0:T(8,128)S(1)}, f32[72,256]{1,0:T(8,128)}, u32[]{:S(2)}) copy-start(f32[72,256]{1,0:T(8,128)} %param.44) | copy-start | bytes 221188
  700.3 22.2 %copy-start.37 = (f32[5896]{0:T(1024)}, f32[5896]{0:T(1024)S(1)}, u32[]{:S(2)}) copy-start(f32[5896]{0:T(1024)S(1)} %get-tuple-element.94) | copy-start | bytes 70756
  701.1 21.4 %copy-start.22 = (f32[3,64,512]{2,1,0:T(8,128)S(1)}, f32[3,64,512]{2,1,0:T(8,128)}, u32[]{:S(2)}) copy-start(f32[3,64,512]{2,1,0:T(8,128)} %param.36) | copy-start | bytes 1179652
  720.1 4.8 copy-start.20
  720.1 4.8 copy-start.23
  722.5 2.4 copy-start.26
  722.5 2.4 copy-start.27
  724.9 1.5 copy-start.33
  724.9 1.5 copy-start.40
  724.9 1.5 copy-start.41
  727.2 5.1 copy-start.19
  731.0 2.8 copy-start.24
  731.0 2.8 copy-start.29
  (11 other events, 9.7 us)
Sparse Core Ops, SparseCore 0:
  10.3 27.8 all-gather.7
  40.4 25.0 all-gather.9
  67.7 31.1 all-gather.5
  327.5 120.3 all-reduce.10
  450.1 38.3 reduce-scatter.1
  495.2 132.2 all-reduce.12
  630.4 42.2 all-reduce.8
  701.2 21.4 all-gather.11

commit v2 on v1

--- a/solution.py
+++ b/solution.py
@@ -150,6 +150,31 @@
         starts.append((start, length))
         start = start + length
     return starts
+
+
+def put_small(ref, index, value):
+    if index < 13:
+        half = value.shape[1]
+        ref[index // 2 : index // 2 + 1, (index % 2) * half : (index % 2 + 1) * half] = value
+    elif index < 16:
+        ref[index - 6 : index - 5, :] = value
+    elif index == 16:
+        half = value.shape[1] // 2
+        ref[10:11, :] = value[:, :half]
+        ref[11:12, :] = value[:, half:]
+    else:
+        ref[index - 5 : index - 4, 0 : value.shape[1]] = value
+
+
+def take_small(rows, latent_ch):
+    return jnp.concatenate(
+        [
+            rows[0:6].reshape(-1),
+            rows[6, : rows.shape[1] // 2],
+            rows[7:12].reshape(-1),
+            rows[12, :latent_ch],
+        ]
+    )
 
 
 def fore_kernel(
@@ -306,6 +331,326 @@
     loop(count, last_part, 0)
 
 
+MESH = pl.DeviceIdType.MESH
+
+
+def places():
+    n_d, n_f = lax.axis_size("dp"), lax.axis_size("fsdp")
+    me = lax.axis_index("fsdp")
+    return n_d, n_f // 2, lax.axis_index("dp"), me // 2, lax.rem(me, 2)
+
+
+def push(src, dst, sends, recvs, target):
+    copy = pltpu.make_async_remote_copy(
+        src_ref=src,
+        dst_ref=dst,
+        send_sem=sends,
+        recv_sem=recvs,
+        device_id=target,
+        device_id_type=MESH,
+    )
+    copy.start()
+    return copy
+
+
+def greet(n_d, n_z, d, z, c):
+    barrier = pltpu.get_barrier_semaphore()
+    for j in range(1, n_d):
+        pl.semaphore_signal(
+            barrier, inc=1, device_id={"dp": lax.rem(d + j, n_d)}, device_id_type=MESH
+        )
+    for k in range(1, n_z):
+        pl.semaphore_signal(
+            barrier,
+            inc=1,
+            device_id={"fsdp": 2 * lax.rem(z + k, n_z) + c},
+            device_id_type=MESH,
+        )
+    pl.semaphore_signal(
+        barrier, inc=1, device_id={"fsdp": 2 * z + 1 - c}, device_id_type=MESH
+    )
+    pl.semaphore_wait(barrier, n_d + n_z - 1)
+
+
+def conv_piece(d, n_d, channels):
+    width = 2 * channels // n_d
+    return (d * width) // channels, pl.ds(
+        pl.multiple_of(lax.rem(d * width, channels), 128), width
+    )
+
+
+def lane_piece(d, n_d, lanes):
+    width = lanes // n_d
+    return pl.ds(pl.multiple_of(d * width, 128), width)
+
+
+def plan_gather(here, parts, wholes, sems):
+    n_d, n_z, d, z, c = here
+    s1, r1, s2, r2, s3, r3 = sems
+    sibling = {"fsdp": 2 * z + 1 - c}
+
+    def copy(ref, sends, recvs, target):
+        return pltpu.make_async_remote_copy(
+            src_ref=ref,
+            dst_ref=ref,
+            send_sem=sends,
+            recv_sem=recvs,
+            device_id=target,
+            device_id_type=MESH,
+        )
+
+    def source(k):
+        return lax.rem(z - k + n_z, n_z)
+
+    def first(k):
+        target = {"fsdp": 2 * lax.rem(z + k, n_z) + c}
+        return [copy(r, s1.at[k, i], r1.at[k, i], target) for i, r in enumerate(parts(z))]
+
+    def second(k, j):
+        target = {"dp": lax.rem(d + j, n_d)}
+        refs = parts(source(k))
+        return [copy(r, s2.at[k, j, i], r2.at[k, j, i], target) for i, r in enumerate(refs)]
+
+    def last(k):
+        refs = wholes(source(k))
+        return [copy(r, s3.at[k, i], r3.at[k, i], sibling) for i, r in enumerate(refs)]
+
+    def start(group):
+        for item in group:
+            item.start()
+
+    def arrive(group):
+        for item in group:
+            item.wait_recv()
+
+    def leave(group):
+        for item in group:
+            item.wait_send()
+
+    far = range(1, n_z)
+    peers = range(1, n_d)
+
+    def step_one():
+        for k in far:
+            start(first(k))
+        start(last(0))
+
+    def step_two():
+        for k in far:
+            arrive(first(k))
+            for j in peers:
+                start(second(k, j))
+
+    def step_three():
+        for k in far:
+            for j in peers:
+                arrive(second(k, j))
+            start(last(k))
+
+    def step_four():
+        for k in range(n_z):
+            arrive(last(k))
+        for k in far:
+            leave(first(k))
+            for j in peers:
+                leave(second(k, j))
+        for k in range(n_z):
+            leave(last(k))
+
+    return step_one, step_two, step_three, step_four
+
+
+def gather_sems(count):
+    n_d, n_z = lax.axis_size("dp"), lax.axis_size("fsdp") // 2
+    dma = pltpu.SemaphoreType.DMA
+    return [
+        dma((n_z, count)),
+        dma((n_z, count)),
+        dma((n_z, n_d, count)),
+        dma((n_z, n_d, count)),
+        dma((n_z, count)),
+        dma((n_z, count)),
+    ]
+
+
+def plan_total(here, value_ref, out, pair, other, from_dp, summed, from_z, sems):
+    n_d, n_z, d, z, c = here
+    lanes_n = out.shape[3]
+    mine = lane_piece(d, n_d, lanes_n)
+    sibling = {"fsdp": 2 * z + 1 - c}
+    send, recv = sems
+
+    def copy(src, dst, index, target):
+        return pltpu.make_async_remote_copy(
+            src_ref=src,
+            dst_ref=dst,
+            send_sem=send.at[index],
+            recv_sem=recv.at[index],
+            device_id=target,
+            device_id_type=MESH,
+        )
+
+    def replica(j):
+        return lax.rem(d + j, n_d)
+
+    def chip(k):
+        return lax.rem(z + k, n_z)
+
+    def one():
+        return [copy(value_ref.at[:, 1 - c], other, 0, sibling)]
+
+    def two():
+        return [
+            copy(
+                pair.at[:, :, lane_piece(replica(j), n_d, lanes_n)],
+                from_dp.at[j],
+                j,
+                {"dp": replica(j)},
+            )
+            for j in range(1, n_d)
+        ]
+
+    def three():
+        return [
+            copy(summed.at[chip(k)], from_z.at[k], n_d + k, {"fsdp": 2 * chip(k) + c})
+            for k in range(1, n_z)
+        ]
+
+    def four():
+        ref = out.at[z, c, :, mine]
+        return [
+            copy(ref, ref, n_d + n_z + j, {"dp": replica(j)}) for j in range(1, n_d)
+        ]
+
+    def five():
+        ref = out.at[z, c]
+        return [
+            copy(ref, ref, 2 * n_d + n_z + k, {"fsdp": 2 * chip(k) + c}) for k in range(1, n_z)
+        ]
+
+    def six():
+        ref = out.at[:, c]
+        return [copy(ref, ref, 2 * n_d + 2 * n_z, sibling)]
+
+    def start(group):
+        for item in group:
+            item.start()
+
+    def arrive(group):
+        for item in group:
+            item.wait_recv()
+
+    def step_one():
+        start(one())
+
+    def step_two():
+        arrive(one())
+        for i in range(n_z):
+            pair[i] = (
+                value_ref[i, pl.ds(c, 1)][0].astype(f32) + other[i].astype(f32)
+            ).astype(pair.dtype)
+        start(two())
+
+    def step_three():
+        arrive(two())
+        for i in range(n_z):
+            value = pair[i, :, mine].astype(f32)
+            for j in range(1, n_d):
+                value = value + from_dp[j, i].astype(f32)
+            summed[i] = value.astype(summed.dtype)
+        start(three())
+
+    def step_four():
+        arrive(three())
+        value = summed[pl.ds(z, 1)][0].astype(f32)
+        for k in range(1, n_z):
+            value = value + from_z[k].astype(f32)
+        out[pl.ds(z, 1), pl.ds(c, 1), :, mine] = value.astype(out.dtype)[None, None]
+        start(four())
+
+    def step_five():
+        arrive(four())
+        start(five())
+
+    def step_six():
+        arrive(five())
+        start(six())
+
+    def step_seven():
+        arrive(six())
+        for group in (one(), two(), three(), four(), five(), six()):
+            for item in group:
+                item.wait_send()
+
+    return step_one, step_two, step_three, step_four, step_five, step_six, step_seven
+
+
+def total_scratch(rows, lanes, dtype):
+    n_d, n_z = lax.axis_size("dp"), lax.axis_size("fsdp") // 2
+    part = lanes // n_d
+    dma = pltpu.SemaphoreType.DMA
+    count = 2 * n_d + 2 * n_z + 1
+    return [
+        pltpu.VMEM((n_z, 2, rows, lanes), dtype),
+        pltpu.VMEM((n_z, rows, lanes), dtype),
+        pltpu.VMEM((n_z, rows, lanes), dtype),
+        pltpu.VMEM((n_d, n_z, rows, part), dtype),
+        pltpu.VMEM((n_z, rows, part), dtype),
+        pltpu.VMEM((n_z, rows, part), dtype),
+        dma((count,)),
+        dma((count,)),
+    ]
+
+
+def fold_rows(value):
+    half = value.shape[0] // 2
+    return jnp.concatenate([value[:half], value[half:]], 1)
+
+
+def shard_gather(here, wide_land, down_land, sems):
+    n_d, n_z, d, z, c = here
+    lanes_w = lane_piece(d, n_d, wide_land.shape[3])
+    lanes_d = lane_piece(d, n_d, down_land.shape[3])
+
+    def parts(source):
+        return [
+            wide_land.at[source, c, :, lanes_w],
+            down_land.at[source, c, :, lanes_d],
+        ]
+
+    def wholes(source):
+        return [wide_land.at[source, c], down_land.at[source, c]]
+
+    return plan_gather(here, parts, wholes, sems)
+
+
+def place_shards(here, wide_ref, down_ref, wide_land, down_land):
+    z, c = here[3], here[4]
+    wide_land[pl.ds(z, 1), pl.ds(c, 1)] = wide_ref[...].astype(bf16)[None, None]
+    down_land[pl.ds(z, 1), pl.ds(c, 1)] = fold_rows(down_ref[...]).astype(bf16)[None, None]
+
+
+def land_out(wide_land, down_land, wide_out, down_out):
+    n_z = wide_land.shape[0]
+    lanes = down_out.shape[1]
+    rows_w, rows_d = wide_land.shape[2], down_land.shape[2]
+    for i in range(n_z):
+        for j in range(2):
+            shard = 2 * i + j
+            wide_out[shard * rows_w : (shard + 1) * rows_w, :] = wide_land[i, j]
+            first = 2 * shard * rows_d
+            down_out[first : first + rows_d, :] = down_land[i, j, :, :lanes]
+            down_out[first + rows_d : first + 2 * rows_d, :] = down_land[i, j, :, lanes:]
+
+
+def land_scratch(wide_shape, down_shape):
+    n_z = lax.axis_size("fsdp") // 2
+    return [
+        pltpu.VMEM((n_z, 2) + wide_shape, bf16),
+        pltpu.VMEM((n_z, 2, down_shape[0] // 2, 2 * down_shape[1]), bf16),
+    ] + gather_sems(2)
+
+
 def fill_query(aug, query, factor, extra):
     dim, length = query.shape
     scaled = query.astype(f32) * (factor * LOG2E)
@@ -339,9 +684,44 @@
 
 
 def attend_kernel(
-    freq_bins, key_block, len_ref, q_ref, k_ref, v_ref, o_ref, lse_ref, kaug, qaug, vaug
+    freq_bins,
+    key_block,
+    len_ref,
+    q_ref,
+    k_ref,
+    v_ref,
+    up_ref,
+    down_ref,
+    o_ref,
+    lse_ref,
+    up_out,
+    down_out,
+    kaug,
+    qaug,
+    vaug,
+    up_land,
+    down_land,
+    *sems,
 ):
     dim, length = q_ref.shape
+    here = places()
+    steps = shard_gather(here, up_land, down_land, sems)
+    head = pl.program_id(0)
+
+    @pl.when(head == 0)
+    def _():
+        place_shards(here, up_ref, down_ref, up_land, down_land)
+        greet(*here)
+        steps[0]()
+
+    pl.when(head == 1)(steps[1])
+    pl.when(head == 3)(steps[2])
+
+    @pl.when(head == 5)
+    def _():
+        steps[3]()
+        land_out(up_land, down_land, up_out, down_out)
+
     live = len_ref[0] * freq_bins
     fill_query(qaug, q_ref[...], dim ** (-0.5), ())
     fill_keys(kaug, k_ref[...], live)
@@ -373,17 +753,66 @@
     lse_ref,
     o_ref,
     do_ref,
+    early_ref,
+    wide_ref,
+    down_ref,
     dq_ref,
     dk_ref,
     dv_ref,
+    early_out,
+    wide_out,
+    down_out,
     kaug,
     qaug,
     vaug,
     daug,
     acc,
+    early_land,
+    pair,
+    other,
+    from_dp,
+    summed,
+    from_z,
+    send,
+    recv,
+    wide_land,
+    down_land,
+    *sems,
 ):
     dim, length = q_ref.shape
     step = pl.program_id(1)
+    here = places()
+    now = pl.program_id(0) * pl.num_programs(1) + step
+    gathers = shard_gather(here, wide_land, down_land, sems)
+    totals = plan_total(
+        here, early_ref, early_land, pair, other, from_dp, summed, from_z, (send, recv)
+    )
+
+    @pl.when(now == 0)
+    def _():
+        place_shards(here, wide_ref, down_ref, wide_land, down_land)
+        greet(*here)
+        totals[0]()
+
+    for place, action in (
+        (2, totals[1]),
+        (6, totals[2]),
+        (9, totals[3]),
+        (11, totals[4]),
+        (13, totals[5]),
+        (16, totals[6]),
+        (17, gathers[0]),
+        (19, gathers[1]),
+        (23, gathers[2]),
+        (27, gathers[3]),
+    ):
+        pl.when(now == place)(action)
+
+    @pl.when(now == 28)
+    def _():
+        early_out[...] = early_land[...]
+        land_out(wide_land, down_land, wide_out, down_out)
+
     factor = dim ** (-0.5)
 
     @pl.when(step == 0)
@@ -424,7 +853,8 @@
     len_ref,
     mixed_ref,
     one_ref,
-    wide_ref,
+    out_ref,
+    up_ref,
     down_ref,
     vec_ref,
     head_ref,
@@ -432,11 +862,8 @@
     noiT_ref,
     two_grad_ref,
     do_ref,
-    gdown_ref,
-    gup_ref,
-    gproj_ref,
+    early_ref,
     ghead_ref,
-    gvec_ref,
     small_ref,
     hidden,
     slope,
@@ -461,7 +888,7 @@
         start, length = segs[index]
         return vec_ref[:, start : start + length]
 
-    w_out = wide_ref[:, 3 * channels : 4 * channels]
+    w_out = out_ref[...]
     proj_bias, gain, shift, up_bias, down_bias = seg(8), seg(9), seg(10), seg(16), seg(11)
 
     def fore(i, carry):
@@ -476,7 +903,7 @@
         spread[rows, :] = jnp.broadcast_to(scale, (CHUNK, spread.shape[1]))
         normed = (hat * gain + shift).astype(bf16)
         normed_t[:, rows] = normed.T
-        pre = mm(normed, wide_ref[:, 4 * channels :]) + up_bias
+        pre = mm(normed, up_ref[...]) + up_bias
         phi = 0.5 * (1.0 + lax.erf(pre * (0.5**0.5)))
         slope[rows, :] = phi + pre * jnp.exp(-0.5 * pre * pre) * (0.5 / math.pi) ** 0.5
         low = (pre * phi).astype(bf16)
@@ -499,12 +926,14 @@
             )
     pos = lax.broadcasted_iota(jnp.int32, predicted.shape, 1)
     errors = jnp.where(pos < live, predicted - noiT_ref[...], 0.0)
-    small_ref[:, 0:128] = jnp.broadcast_to(
-        jnp.sum(errors, axis=1, keepdims=True), (latent_ch, 128)
-    )
-    small_ref[:, 128:256] = jnp.broadcast_to(
-        jnp.sum(errors * errors, axis=1, keepdims=True), (latent_ch, 128)
-    )
+    small_ref[...] = jnp.zeros(small_ref.shape, f32)
+    tile = (latent_ch, 128)
+    sums = jnp.broadcast_to(jnp.sum(errors, axis=1, keepdims=True), tile)
+    same = lax.broadcasted_iota(jnp.int32, tile, 0) == lax.broadcasted_iota(jnp.int32, tile, 1)
+    put_small(small_ref, 17, col_sum(jnp.where(same, sums, 0.0)))
+    sums = jnp.broadcast_to(jnp.sum(errors * errors, axis=1, keepdims=True), tile)
+    put_small(small_ref, 18, col_sum(sums))
+    put_small(small_ref, 19, jnp.zeros((1, 128), f32) + live.astype(f32))
     errors = errors.astype(bf16).astype(f32)
     for a in range(3):
         for b in range(3):
@@ -527,7 +956,7 @@
         pre = mm_nt(low, down_ref[...]) * slope[rows, :]
         pre_low = pre.astype(bf16)
         gpre[rows, :] = pre_low
-        dnormed = mm_nt(pre_low, wide_ref[:, 4 * channels :])
+        dnormed = mm_nt(pre_low, up_ref[...])
         hat = xhat[rows, :]
         dhat = dnormed * gain
         dstream = (dhat - row_mean(dhat) - hat * row_mean(dhat * hat)) * spread[rows, 0:1]
@@ -546,15 +975,25 @@
 
     blank = jnp.zeros((1, channels), f32)
     sums = loop(count, back, (blank, jnp.zeros((1, units), f32), blank, blank, blank))
-    gvec_ref[...] = jnp.zeros(gvec_ref.shape, f32)
     for index, value in zip((11, 16, 9, 10, 8), sums):
-        start, length = segs[index]
-        gvec_ref[:, start : start + length] = value
-    gproj_ref[...] = mm(mixed_ref[...].astype(bf16), glow[...]).astype(bf16)
+        put_small(small_ref, index, value)
+    half = units // 2
     for part in range(units // channels):
         columns = slice(part * channels, (part + 1) * channels)
-        gdown_ref[columns, :] = mm(three_t[...], hidden[:, columns]).T.astype(bf16)
-        gup_ref[:, columns] = mm(normed_t[...], gpre[:, columns]).astype(bf16)
+        first = (part * channels) % half
+        lanes = slice((part * channels) // half * channels, (part * channels) // half * channels + channels)
+        early_ref[first : first + channels, lanes] = mm(three_t[...], hidden[:, columns]).T.astype(
+            bf16
+        )
+        first = half + (part // 2) * channels
+        lanes = slice((part % 2) * channels, (part % 2 + 1) * channels)
+        early_ref[first : first + channels, lanes] = mm(normed_t[...], gpre[:, columns]).astype(
+            bf16
+        )
+    gproj = mm(mixed_ref[...].astype(bf16), glow[...]).astype(bf16)
+    first = half + (units // channels // 2) * channels
+    early_ref[first:, 0:channels] = gproj[: channels // 2]
+    early_ref[first:, channels:] = gproj[channels // 2 :]
 
 
 def hind_kernel(
@@ -579,15 +1018,17 @@
     time_ref,
     vec_ref,
     wave_ref,
+    mid_ref,
+    ghead_ref,
     gqkv_ref,
     gconv_ref,
-    gstem_ref,
-    gvec_ref,
+    gsmall_ref,
     factor_ref,
     buf,
     field,
     other,
     act_t,
+    small,
 ):
     rows_n, channels = one_ref.shape
     embed = time_ref.shape[1]
@@ -597,19 +1038,21 @@
     counted = (live * (channels // groups)).astype(f32)
     segs = offsets(channels, embed, FF, latent_ch)
     blank = jnp.zeros((1, channels), f32)
-    gvec_ref[...] = jnp.zeros(gvec_ref.shape, f32)
+    small[...] = jnp.zeros(small.shape, f32)
 
     def seg(index):
         start, length = segs[index]
         return vec_ref[:, start : start + length]
 
     def put_vec(index, value):
-        start, length = segs[index]
-        gvec_ref[:, start : start + length] = value
-
-    for part, ref in enumerate((dq_ref, dk_ref, dv_ref)):
-        columns = slice(part * channels, (part + 1) * channels)
-        gqkv_ref[:, columns] = mm(ref[...], normed_ref[...]).T.astype(bf16)
+        put_small(small, index, value)
+
+    half = channels // 2
+    gqkv_ref[0:channels, 0:channels] = mm(dq_ref[...], normed_ref[...]).T.astype(bf16)
+    gqkv_ref[0:channels, channels:] = mm(dk_ref[...], normed_ref[...]).T.astype(bf16)
+    values_grad = mm(dv_ref[...], normed_ref[...]).T.astype(bf16)
+    gqkv_ref[channels:, 0:channels] = values_grad[:half]
+    gqkv_ref[channels:, channels:] = values_grad[half:]
 
     gain_one = seg(6)
     clear_ends(buf, rows_n, freq_bins)
@@ -745,7 +1188,9 @@
     g_stem, g_bias = loop(
         count, zero_part, (jnp.zeros((colsT_ref.shape[0], channels), f32), blank)
     )
-    gstem_ref[...] = g_stem
+    taps = colsT_ref.shape[0]
+    gsmall_ref[0:taps, 0:channels] = g_stem
+    gsmall_ref[0:taps, channels:] = ghead_ref[...]
     put_vec(12, g_bias)
 
     pre_time = film_ref[1:2]
@@ -756,6 +1201,10 @@
     put_vec(13, g_time)
     put_vec(14, g_embed)
     put_vec(15, g_film)
+    gsmall_ref[taps : taps + 16, :] = small[...] + mid_ref[...]
+    gsmall_ref[taps + 16 :, :] = jnp.zeros(
+        (gsmall_ref.shape[0] - taps - 16, gsmall_ref.shape[1]), f32
+    )
     factor_ref[0:1] = wave_ref[...]
     factor_ref[1:2] = jax.nn.silu(pre_time)
     factor_ref[2:3] = jax.nn.silu(embedding)
@@ -775,6 +1224,12 @@
 
 def params(mib):
     return pltpu.CompilerParams(vmem_limit_bytes=mib * 2**20)
+
+
+def remote_params(number, mib):
+    return pltpu.CompilerParams(
+        collective_id=number, has_side_effects=True, vmem_limit_bytes=mib * 2**20
+    )
 
 
 def run_fore(freq_bins, length, mix, lat, noi, stem_w, conv, wide_qkv, time_low, vec, wave, clap):
@@ -810,7 +1265,8 @@
     )(length, mix, lat, noi, stem_w, conv, wide_qkv, time_low, vec, wave, clap)
 
 
-def run_attend(freq_bins, length, qkv_t, key_block=256):
+def run_attend(freq_bins, length, qkv_t, up, down, key_block=256):
+    n_f = lax.axis_size("fsdp")
     triple, rows_n = qkv_t.shape
     channels = triple // 3
     dim = channels // HEADS
@@ -818,23 +1274,36 @@
         functools.partial(attend_kernel, freq_bins, key_block),
         grid=(HEADS,),
         in_specs=[SM]
-        + [pl.BlockSpec((dim, rows_n), lambda h, t=t: (t * HEADS + h, 0)) for t in range(3)],
+        + [pl.BlockSpec((dim, rows_n), lambda h, t=t: (t * HEADS + h, 0)) for t in range(3)]
+        + [VM] * 2,
         out_specs=[
             pl.BlockSpec((dim, rows_n), lambda h: (h, 0)),
             pl.BlockSpec((1, 1, rows_n), lambda h: (h, 0, 0)),
+            VM,
+            VM,
         ],
-        out_shape=[sized((channels, rows_n)), sized((HEADS, 1, rows_n))],
+        out_shape=[
+            sized((channels, rows_n)),
+            sized((HEADS, 1, rows_n)),
+            sized((up.shape[0] * n_f, up.shape[1]), bf16),
+            sized((down.shape[0] * n_f, down.shape[1]), bf16),
+        ],
         scratch_shapes=[
             pltpu.VMEM((rows_n, 128), bf16),
             pltpu.VMEM((128, rows_n), bf16),
             pltpu.VMEM((dim + 16, rows_n), bf16),
-        ],
-        compiler_params=params(48),
+        ]
+        + land_scratch(up.shape, down.shape),
+        compiler_params=remote_params(3, 48),
         name="attend",
-    )(length, qkv_t, qkv_t, qkv_t)
-
-
-def run_attend_back(freq_bins, length, qkv_t, lse, mixed_t, grad_t, key_block=512):
+    )(length, qkv_t, qkv_t, qkv_t, up, down)
+
+
+def run_attend_back(
+    freq_bins, length, qkv_t, lse, mixed_t, grad_t, early, wide, down, key_block=512
+):
+    n_f = lax.axis_size("fsdp")
+    early = early.reshape(n_f // 2, 2, early.shape[0] // n_f, early.shape[1])
     triple, rows_n = qkv_t.shape
     channels = triple // 3
     dim = channels // HEADS
@@ -845,38 +1314,43 @@
         grid=(HEADS, rows_n // key_block),
         in_specs=[SM]
         + [pl.BlockSpec((dim, rows_n), lambda h, j, t=t: (t * HEADS + h, 0)) for t in range(3)]
-        + [pl.BlockSpec((1, 1, rows_n), lambda h, j: (h, 0, 0)), whole, whole],
-        out_specs=[whole, block, block],
-        out_shape=[sized((channels, rows_n), bf16)] * 3,
+        + [pl.BlockSpec((1, 1, rows_n), lambda h, j: (h, 0, 0)), whole, whole]
+        + [VM] * 3,
+        out_specs=[whole, block, block] + [VM] * 3,
+        out_shape=[sized((channels, rows_n), bf16)] * 3
+        + [
+            sized(early.shape, bf16),
+            sized((wide.shape[0] * n_f, wide.shape[1]), bf16),
+            sized((down.shape[0] * n_f, down.shape[1]), bf16),
+        ],
         scratch_shapes=[
             pltpu.VMEM((rows_n, 128), bf16),
             pltpu.VMEM((128, rows_n), bf16),
             pltpu.VMEM((rows_n, 128), bf16),
             pltpu.VMEM((128, rows_n), bf16),
             pltpu.VMEM((dim, rows_n), f32),
-        ],
-        compiler_params=params(48),
+        ]
+        + total_scratch(early.shape[2], early.shape[3], bf16)
+        + land_scratch(wide.shape, down.shape),
+        compiler_params=remote_params(4, 56),
         name="attend_back",
-    )(length, qkv_t, qkv_t, qkv_t, lse, mixed_t, grad_t)
-
-
-def run_middle(freq_bins, length, mixed_t, one, wide, down, vec, head_t, head_bias, noi_t):
+    )(length, qkv_t, qkv_t, qkv_t, lse, mixed_t, grad_t, early, wide, down)
+
+
+def run_middle(freq_bins, length, mixed_t, one, out, up, down, vec, head_t, head_bias, noi_t):
     rows_n, channels = one.shape
     units = down.shape[0]
     latent_ch = noi_t.shape[0]
     return pl.pallas_call(
         functools.partial(middle_kernel, freq_bins),
-        in_specs=[SM] + [VM] * 8,
-        out_specs=[VM] * 8,
+        in_specs=[SM] + [VM] * 9,
+        out_specs=[VM] * 5,
         out_shape=[
             sized((rows_n, channels)),
             sized((channels, rows_n), bf16),
-            sized((units, channels), bf16),
-            sized((channels, units), bf16),
-            sized((channels, channels), bf16),
+            sized((units + channels // 2, 2 * channels), bf16),
             sized((9 * latent_ch, channels)),
-            sized(vec.shape),
-            sized((latent_ch, 256)),
+            sized((16, 2 * channels)),
         ],
         scratch_shapes=[
             pltpu.VMEM((rows_n, units), bf16),
@@ -893,24 +1367,21 @@
         ],
         compiler_params=params(56),
         name="middle",
-    )(length, mixed_t, one, wide, down, vec, head_t, head_bias, noi_t)
+    )(length, mixed_t, one, out, up, down, vec, head_t, head_bias, noi_t)
 
 
 def run_hind(freq_bins, length, *arrays):
     one = arrays[5]
     rows_n, channels = one.shape
-    cols_t = arrays[10]
-    vec = arrays[16]
     embed = arrays[15].shape[1]
     return pl.pallas_call(
         functools.partial(hind_kernel, freq_bins, GROUPS),
         in_specs=[SM] + [VM] * len(arrays),
-        out_specs=[VM] * 5,
+        out_specs=[VM] * 4,
         out_shape=[
-            sized((channels, 3 * channels), bf16),
+            sized((channels + channels // 2, 2 * channels), bf16),
             sized((2, 9 * channels, channels), bf16),
-            sized((cols_t.shape[0], channels)),
-            sized(vec.shape),
+            sized((128, 2 * channels)),
             sized((8, embed)),
         ],
         scratch_shapes=[
@@ -918,10 +1389,364 @@
             pltpu.VMEM((rows_n, channels), f32),
             pltpu.VMEM((rows_n, channels), f32),
             pltpu.VMEM((channels, rows_n), bf16),
+            pltpu.VMEM((16, 2 * channels), f32),
         ],
         compiler_params=params(56),
         name="hind",
     )(length, *arrays)
+
+
+def gather_kernel(conv_ref, time_ref, wide_ref, conv_out, time_out, wide_out, *sems):
+    here = places()
+    n_d, n_z, d, z, c = here
+    channels, embed = conv_ref.shape[2], time_ref.shape[2]
+    which, lanes = conv_piece(d, n_d, channels)
+    t_lanes = lane_piece(d, n_d, embed)
+    w_lanes = lane_piece(d, n_d, wide_out.shape[3])
+    conv_out[:, pl.ds(z, 1), pl.ds(c, 1)] = conv_ref[...].astype(bf16)[:, None, None]
+    time_out[:, pl.ds(z, 1), pl.ds(c, 1)] = time_ref[...].astype(bf16)[:, None, None]
+    wide_out[pl.ds(z, 1), pl.ds(c, 1)] = wide_ref[...].astype(bf16)[None, None]
+
+    def parts(source):
+        return [
+            conv_out.at[which, source, c, :, lanes],
+            time_out.at[:, source, c, :, t_lanes],
+            wide_out.at[source, c, :, w_lanes],
+        ]
+
+    def wholes(source):
+        return [
+            conv_out.at[:, source, c],
+            time_out.at[:, source, c],
+            wide_out.at[source, c],
+        ]
+
+    steps = plan_gather(here, parts, wholes, sems)
+    greet(*here)
+    for step in steps:
+        step()
+
+
+def run_gather(conv_w, time_w, wide):
+    n_z = lax.axis_size("fsdp") // 2
+    conv, time, wide_full = pl.pallas_call(
+        gather_kernel,
+        in_specs=[VM] * 3,
+        out_specs=[VM] * 3,
+        out_shape=[
+            sized((2, n_z, 2) + conv_w.shape[1:], bf16),
+            sized((3, n_z, 2) + time_w.shape[1:], bf16),
+            sized((n_z, 2) + wide.shape, bf16),
+        ],
+        scratch_shapes=gather_sems(3),
+        compiler_params=remote_params(1, 32),
+        name="gather",
+    )(conv_w, time_w, wide)
+    return (
+        conv.reshape(2, -1, conv_w.shape[2]),
+        time.reshape(3, -1, time_w.shape[2]),
+        wide_full.reshape(-1, wide.shape[1]),
+    )
+
+
+def reduce_kernel(
+    gconv_ref,
+    ga_ref,
+    gs_ref,
+    factor_ref,
+    conv_out,
+    a_out,
+    s_out,
+    time_out,
+    square_out,
+    shard,
+    pair_c,
+    pair_a,
+    pair_s,
+    sib_c,
+    sib_a,
+    sib_s,
+    dp_c,
+    dp_a,
+    dp_s,
+    sum_c,
+    sum_a,
+    sum_s,
+    z_c,
+    z_a,
+    z_s,
+    everyone,
+    squares,
+    product,
+    s1,
+    r1,
+    s2,
+    r2,
+    s3,
+    r3,
+    s4,
+    r4,
+    s5,
+    r5,
+    s6,
+    r6,
+):
+    n_d, n_z, d, z, c = places()
+    rows_here, channels = conv_out.shape[1:]
+    wide = a_out.shape[3]
+    embed = factor_ref.shape[1]
+    which, lanes = conv_piece(d, n_d, channels)
+    a_lanes = lane_piece(d, n_d, wide)
+    sibling = {"fsdp": 2 * z + 1 - c}
+    everyone[pl.ds(d, 1), pl.ds(z, 1), pl.ds(c, 1)] = factor_ref[...][None, None, None]
+    greet(n_d, n_z, d, z, c)
+    copies = []
+
+    def send(pairs, sends, recvs, target):
+        group = []
+        for index, (src, dst) in enumerate(pairs):
+            group.append(push(src, dst, sends.at[index], recvs.at[index], target))
+        copies.extend(group)
+        return group
+
+    def arrive(groups):
+        for group in groups:
+            for copy in group:
+                copy.wait_recv()
+
+    one = send(
+        (
+            (gconv_ref.at[:, :, 1 - c], sib_c),
+            (ga_ref.at[:, 1 - c], sib_a),
+            (gs_ref.at[:, 1 - c], sib_s),
+        ),
+        s1,
+        r1,
+        sibling,
+    )
+    mine = everyone.at[d, z, c]
+    two_f = [
+        send(((mine, mine),), s2.at[j, 3:4], r2.at[j, 3:4], {"dp": lax.rem(d + j, n_d)})
+        for j in range(1, n_d)
+    ]
+    arrive([one])
+    for i in range(n_z):
+        for part in range(2):
+            pair_c[part, i] = (
+                gconv_ref[part, i, pl.ds(c, 1)][0].astype(f32) + sib_c[part, i].astype(f32)
+            ).astype(bf16)
+        pair_a[i] = (ga_ref[i, pl.ds(c, 1)][0].astype(f32) + sib_a[i].astype(f32)).astype(bf16)
+        pair_s[i] = gs_ref[i, pl.ds(c, 1)][0] + sib_s[i]
+
+    two = []
+    for j in range(1, n_d):
+        other = lax.rem(d + j, n_d)
+        other_which, other_lanes = conv_piece(other, n_d, channels)
+        other_a = lane_piece(other, n_d, wide)
+        two.append(
+            send(
+                (
+                    (pair_c.at[other_which, :, :, other_lanes], dp_c.at[j]),
+                    (pair_a.at[:, :, other_a], dp_a.at[j]),
+                    (pair_s.at[:, :, other_a], dp_s.at[j]),
+                ),
+                s2.at[j],
+                r2.at[j],
+                {"dp": other},
+            )
+        )
+    arrive(two_f)
+    column = everyone.at[:, z, c]
+    three_f = [
+        send(
+            ((column, column),),
+            s3.at[k, 3:4],
+            r3.at[k, 3:4],
+            {"fsdp": 2 * lax.rem(z + k, n_z) + c},
+        )
+        for k in range(1, n_z)
+    ]
+    arrive(two)
+
+    def total(first, rest):
+        value = first.astype(f32)
+        for term in rest:
+            value = value + term.astype(f32)
+        return value
+
+    for i in range(n_z):
+        rest = range(1, n_d)
+        sum_c[i] = total(
+            pair_c[pl.ds(which, 1), i, :, lanes][0], [dp_c[j, i] for j in rest]
+        ).astype(bf16)
+        sum_a[i] = total(pair_a[i, :, a_lanes], [dp_a[j, i] for j in rest]).astype(bf16)
+        sum_s[i] = total(pair_s[i, :, a_lanes], [dp_s[j, i] for j in rest])
+
+    three = []
+    for k in range(1, n_z):
+        other = lax.rem(z + k, n_z)
+        three.append(
+            send(
+                (
+                    (sum_c.at[other], z_c.at[k]),
+                    (sum_a.at[other], z_a.at[k]),
+                    (sum_s.at[other], z_s.at[k]),
+                ),
+                s3.at[k],
+                r3.at[k],
+                {"fsdp": 2 * other + c},
+            )
+        )
+    arrive(three_f)
+    row = everyone.at[:, :, c]
+    four_f = send(((row, row),), s4.at[0], r4.at[0], sibling)
+    arrive(three)
+    rest = range(1, n_z)
+    shard[pl.ds(which, 1), :, lanes] = total(
+        sum_c[pl.ds(z, 1)][0], [z_c[k] for k in rest]
+    ).astype(bf16)[None]
+    a_out[pl.ds(z, 1), pl.ds(c, 1), :, a_lanes] = total(
+        sum_a[pl.ds(z, 1)][0], [z_a[k] for k in rest]
+    ).astype(bf16)[None, None]
+    s_out[pl.ds(z, 1), pl.ds(c, 1), :, a_lanes] = total(
+        sum_s[pl.ds(z, 1)][0], [z_s[k] for k in rest]
+    )[None, None]
+
+    four = []
+    for j in range(1, n_d):
+        refs = (
+            shard.at[which, :, lanes],
+            a_out.at[z, c, :, a_lanes],
+            s_out.at[z, c, :, a_lanes],
+        )
+        four.append(
+            send(
+                [(ref, ref) for ref in refs],
+                s4.at[j],
+                r4.at[j],
+                {"dp": lax.rem(d + j, n_d)},
+            )
+        )
+    arrive([four_f])
+    clips = 2 * n_d * n_z
+    depth = time_out.shape[1]
+    first = (2 * z + c) * depth
+    block = pl.ds(pl.multiple_of(first // 128 * 128, 128), 128)
+    offset = pl.multiple_of(lax.rem(first, 128), 8)
+    square = jnp.zeros((), f32)
+    for i in range(3):
+        left = everyone[:, :, :, i, block].reshape(clips, 128)
+        right = everyone[:, :, :, i + 3, :].reshape(clips, embed)
+        product[...] = jnp.dot(
+            left.T, right, precision=highest, preferred_element_type=f32
+        )
+        value = product[pl.ds(offset, depth), :]
+        time_out[i] = value
+        square = square + jnp.sum(value * value)
+    arrive(four)
+    value = shard[...].astype(f32)
+    conv_out[...] = value
+    square = square + jnp.sum(value * value)
+    squares[pl.ds(z, 1), pl.ds(c, 1)] = jnp.zeros((1, 1) + squares.shape[2:], f32) + square
+
+    five = []
+    for k in range(1, n_z):
+        refs = (a_out.at[z, c], s_out.at[z, c], squares.at[z, c])
+        five.append(
+            send(
+                [(ref, ref) for ref in refs],
+                s5.at[k],
+                r5.at[k],
+                {"fsdp": 2 * lax.rem(z + k, n_z) + c},
+            )
+        )
+    arrive(five)
+    refs = (a_out.at[:, c], s_out.at[:, c], squares.at[:, c])
+    six = send([(ref, ref) for ref in refs], s6, r6, sibling)
+    arrive([six])
+    value = jnp.zeros(squares.shape[2:], f32)
+    for i in range(n_z):
+        for j in range(2):
+            value = value + squares[i, j]
+    square_out[...] = value
+    for copy in copies:
+        copy.wait_send()
+
+
+def run_reduce(gconv, ga, gs, factors, time_rows):
+    n_d, n_f = lax.axis_size("dp"), lax.axis_size("fsdp")
+    n_z = n_f // 2
+    channels = gconv.shape[2]
+    embed = factors.shape[1]
+    rows_c = gconv.shape[1] // n_f
+    rows_a = ga.shape[0] // n_f
+    rows_s = gs.shape[0] // n_f
+    wide = ga.shape[1]
+    part = wide // n_d
+    part_c = 2 * channels // n_d
+    dma = pltpu.SemaphoreType.DMA
+    vmem = pltpu.VMEM
+    conv, a_full, s_full, time, square = pl.pallas_call(
+        reduce_kernel,
+        in_specs=[VM] * 4,
+        out_specs=[VM] * 5,
+        out_shape=[
+            sized((2, rows_c, channels)),
+            sized((n_z, 2, rows_a, wide), bf16),
+            sized((n_z, 2, rows_s, wide)),
+            sized((3, time_rows, embed)),
+            sized((8, 128)),
+        ],
+        scratch_shapes=[
+            vmem((2, rows_c, channels), bf16),
+            vmem((2, n_z, rows_c, channels), bf16),
+            vmem((n_z, rows_a, wide), bf16),
+            vmem((n_z, rows_s, wide), f32),
+            vmem((2, n_z, rows_c, channels), bf16),
+            vmem((n_z, rows_a, wide), bf16),
+            vmem((n_z, rows_s, wide), f32),
+            vmem((n_d, n_z, rows_c, part_c), bf16),
+            vmem((n_d, n_z, rows_a, part), bf16),
+            vmem((n_d, n_z, rows_s, part), f32),
+            vmem((n_z, rows_c, part_c), bf16),
+            vmem((n_z, rows_a, part), bf16),
+            vmem((n_z, rows_s, part), f32),
+            vmem((n_z, rows_c, part_c), bf16),
+            vmem((n_z, rows_a, part), bf16),
+            vmem((n_z, rows_s, part), f32),
+            vmem((n_d, n_z, 2, 8, embed), f32),
+            vmem((n_z, 2, 8, 128), f32),
+            vmem((128, embed), f32),
+            dma((3,)),
+            dma((3,)),
+            dma((n_d, 4)),
+            dma((n_d, 4)),
+            dma((n_z, 4)),
+            dma((n_z, 4)),
+            dma((n_d, 3)),
+            dma((n_d, 3)),
+            dma((n_z, 3)),
+            dma((n_z, 3)),
+            dma((3,)),
+            dma((3,)),
+        ],
+        compiler_params=pltpu.CompilerParams(
+            collective_id=2, has_side_effects=True, vmem_limit_bytes=48 * 2**20
+        ),
+        name="reduce",
+    )(
+        gconv.reshape(2, n_z, 2, rows_c, channels),
+        ga.reshape(n_z, 2, rows_a, wide),
+        gs.reshape(n_z, 2, rows_s, wide),
+        factors,
+    )
+    return (
+        conv,
+        a_full.reshape(ga.shape),
+        s_full.reshape(gs.shape),
+        time,
+        square[0, 0],
+    )
 
 
 def noise_mix(step_value):
@@ -974,15 +1799,7 @@
     both = ("dp", "fsdp")
     here = lax.axis_index("fsdp")
 
-    def gather(value, dim):
-        return lax.all_gather(value.astype(bf16), "fsdp", axis=dim, tiled=True)
-
-    conv_full = gather(conv_w, 1)
-    time_full = gather(time_w, 1)
-    wide_full = gather(wide_w, 0)
-    down_full = gather(down_w, 0)
-    wide_moment_full = gather(wide_moment, 0)
-    down_moment_full = gather(down_moment, 0)
+    conv_full, time_full, first_full = run_gather(conv_w, time_w, wide_w[:, : 4 * channels])
 
     half_width = embed // 2
     frequency = jnp.exp(-math.log(10000.0) * jnp.arange(half_width).astype(f32) / half_width)
@@ -1015,19 +1832,41 @@
         noises.reshape(rows_n, latent_ch),
         stem_w,
         conv_full,
-        wide_full[:, : 3 * channels],
+        first_full[:, : 3 * channels],
         time_full,
         vec,
         wave,
         clap_embed,
     )
-    mixed_t, lse = run_attend(freq_bins, lengths, qkv_t)
-    two_grad, do_t, gdown, gup, gproj, ghead_t, gvec_mid, small = run_middle(
-        freq_bins, lengths, mixed_t, one, wide_full, down_full, vec, head_t, head_bias, noi_t
-    )
-    gdown, gup, gproj = lax.psum((gdown, gup, gproj), both)
-    dq, dk, dv = run_attend_back(freq_bins, lengths, qkv_t, lse, mixed_t, do_t)
-    gqkv, gconv, gstem, gvec_hind, factors = run_hind(
+    mixed_t, lse, up_full, down_full = run_attend(
+        freq_bins, lengths, qkv_t, wide_w[:, 4 * channels :], down_w
+    )
+    two_grad, do_t, early, ghead_t, small = run_middle(
+        freq_bins,
+        lengths,
+        mixed_t,
+        one,
+        first_full[:, 3 * channels :],
+        up_full,
+        down_full,
+        vec,
+        head_t,
+        head_bias,
+        noi_t,
+    )
+    dq, dk, dv, early, wide_moment_full, down_moment_full = run_attend_back(
+        freq_bins, lengths, qkv_t, lse, mixed_t, do_t, early, wide_moment, down_moment
+    )
+    early = early.reshape(-1, early.shape[3])
+    half = FF // 2
+    gdown = jnp.concatenate([early[:half, :channels], early[:half, channels:]], 0)
+    gup = jnp.concatenate(
+        [early[half : half + channels], early[half + channels : half + 2 * channels]], 1
+    )
+    gproj = jnp.concatenate(
+        [early[half + 2 * channels :, :channels], early[half + 2 * channels :, channels:]], 0
+    )
+    ga, gconv, gs, factors = run_hind(
         freq_bins,
         lengths,
         dq,
@@ -1044,33 +1883,39 @@
         stat,
         film,
         conv_full,
-        wide_full,
+        first_full,
         time_full,
         vec,
         wave,
-    )
-
-    conv_shard = lax.psum_scatter(gconv, "fsdp", scatter_dimension=1, tiled=True)
-    conv_shard = lax.psum(conv_shard, "dp").astype(f32)
-    gqkv = lax.psum(gqkv, both)
-    gvec_head = jnp.pad(small[:, 0], (vector.shape[0] - latent_ch, 0))
-    gvec = gvec_mid[0] + gvec_hind[0] + gvec_head
-    loss_local = jnp.sum(small[:, 128])
-    live_local = lengths[0].astype(f32) * freq_bins
-    loss_sum, live_count, gstem, ghead_t, gvec = lax.psum(
-        (loss_local, live_local, gstem, ghead_t, gvec), both
-    )
-    ghead = ghead_t.reshape(9, latent_ch, channels).transpose(0, 2, 1).reshape(-1, latent_ch)
-    everyone = lax.all_gather(factors, both, axis=0)
-    rows_here = time_w.shape[1]
-    sides = lax.dynamic_slice_in_dim(everyone[:, 0:3], here * rows_here, rows_here, 2)
-    time_shard = jnp.einsum("niw,niv->iwv", sides, everyone[:, 3:6], precision=highest)
+        small,
+        ghead_t,
+    )
+    conv_shard, ga, gs, time_shard, shard_total = run_reduce(
+        gconv, ga, gs, factors, time_w.shape[1]
+    )
+    gqkv = jnp.concatenate(
+        [
+            ga[:channels],
+            jnp.concatenate([ga[channels:, :channels], ga[channels:, channels:]], 0),
+        ],
+        1,
+    )
+    taps = stem_w.shape[0]
+    gstem = gs[:taps, :channels]
+    ghead = (
+        gs[:taps, channels:]
+        .reshape(9, latent_ch, channels)
+        .transpose(0, 2, 1)
+        .reshape(-1, latent_ch)
+    )
+    gvec = take_small(gs[taps:], latent_ch)
+    loss_sum = gs[taps + 13, 0]
+    live_count = gs[taps + 14, 0]
 
     def squares(value):
         value = value.astype(f32)
         return jnp.sum(value * value)
 
-    shard_total = lax.psum(squares(conv_shard) + squares(time_shard), "fsdp")
     total = (
         shard_total
         + squares(gstem)

time: 745 us -> 392 us (0.53)
  waiting for transfers between devices: 305 us -> 0 us
  blocking collectives: 135 us -> 0 us
  Pallas kernels: 216 us -> 323 us
  between operations: 26.9 us -> 12.2 us
  other arithmetic: 29.1 us -> 17.3 us
    psum x3 -> x0, waiting for transfers between devices: 205 us -> none  [the longest x1 139 us: local(): gdown, gup, gproj = lax.psum((gdown, gup, gproj), both)]
    pallas_call x0 -> x2, Pallas kernels: none -> 82.1 us  [the longest x1 49.7 us: run_reduce(): pl.pallas_call(reduce_kernel, in_specs=[VM] * 4, out_specs=[VM] * 5, out_...]
    all_gather x3 -> x0, blocking collectives: 78.1 us -> none  [the longest x1 41.8 us: local(): everyone = lax.all_gather(factors, both, axis=0)]
    all_gather x4 -> x0, waiting for transfers between devices: 61.9 us -> none  [gather(): return lax.all_gather(value.astype(bf16), 'fsdp', axis=dim, tiled=True)]
    psum x2 -> x0, blocking collectives: 57.3 us -> none  [the longest x1 40.8 us: local(): lax.psum((loss_local, live_local, gstem, ghead_t, gvec), both)]
    reduce_scatter x1 -> x0, waiting for transfers between devices: 37.6 us -> none  [local(): lax.psum_scatter(gconv, 'fsdp', scatter_dimension=1, tiled=True)]
    pallas_call x1, Pallas kernels: 95.5 us -> 113 us  [run_attend_back(): pl.pallas_call(functools.partial(attend_back_kernel, freq_bins, key_block...]
    reduce_sum x8 -> x6, other arithmetic: 12.7 us -> 4.43 us  [squares(): return jnp.sum(value * value)]
  transfers between devices with their start and end apart: 8 -> 0, of which waited for: 7 -> 0; matrix products, arithmetic and copies ran while one was open for 4% -> 0% of each run, Pallas kernels for 0% -> 0%
where the time goes in v2:
time: 392 us; the launch traced here: 391 us
  Pallas kernels  323 us (82%)
  local copies, waits for them, and re-layouts  28.4 us (7%)
  other arithmetic  17.3 us (4%)
  between operations  12.2 us (3%)
  matrix products  9.64 us (2%)
    pallas_call x1, Pallas kernels, run_attend_back(): pl.pallas_call(functools.partial(attend_back_kernel, freq_bins, key_block...  113 us
    pallas_call x1, Pallas kernels, run_reduce(): pl.pallas_call(reduce_kernel, in_specs=[VM] * 4, out_specs=[VM] * 5, out_...  49.7 us
    pallas_call x1, Pallas kernels, run_attend(): pl.pallas_call(functools.partial(attend_kernel, freq_bins, key_block), gr...  43.9 us
    pallas_call x1, Pallas kernels, run_hind(): pl.pallas_call(functools.partial(hind_kernel, freq_bins, GROUPS), in_spec...  33.2 us
    pallas_call x1, Pallas kernels, run_gather(): pl.pallas_call(gather_kernel, in_specs=[VM] * 3, out_specs=[VM] * 3, out_...  32.4 us
    pallas_call x1, Pallas kernels, run_fore(): pl.pallas_call(functools.partial(fore_kernel, freq_bins, GROUPS), in_spec...  25.8 us
    pallas_call x1, Pallas kernels, run_middle(): pl.pallas_call(functools.partial(middle_kernel, freq_bins), in_specs=[SM]...  25.1 us
    unnamed x98, local copies, waits for them, and re-layouts  18.4 us

profile of v2, /device:TPU:0, one launch (start us, length us, event | category | flops | bytes accessed | tf_op | source)
XLA Modules:
  0.0 390.6 jit_solution(15261705593067441536)
XLA Ops:
  0.7 1.0 fusion.106
  1.8 1.1 copy-done.3
  2.8 1.0 copy-done.7
  3.8 32.4 %gather.1 = (bf16[2,4,2,288,256]{4,3,2,1,0:T(8,128)(2,1)S(1)}, bf16[3,4,2,64,512]{4,3,2,1,0:T(8,128)(2,1)S(1)}, bf16[4,2,32,1024]{3,2,1,0:T(8,128)(2,1)S(1)}) custom-call(f32[2,288,256]{2,1,0:T(8,128)S(1)} %copy-done.3, f32[3,64,512]{2,1,0:T(8,128)S(1)} %copy-done.7, f32[32,1024]{1,0:T(8,128)S(1)} %get-tuple-element.131.wide_ref), custom_call_target="tpu_custom_call" | custom-call | tf_op jit(solution)/shard_map/gather/pallas_call | solution.py:1432
  36.2 1.4 copy-done
  37.6 1.2 copy-done.2
  41.4 25.8 %fore.1 = (f32[2048,256]{1,0:T(8,128)}, bf16[2048,256]{1,0:T(8,128)(2,1)S(1)}, f32[2048,256]{1,0:T(8,128)}, bf16[2048,256]{1,0:T(8,128)(2,1)S(1)}, f32[2048,256]...) custom-call(s32[1]{0:T(128)S(6)} %copy.57.len_ref, ...), custom_call_target="tpu_custom_call" | custom-call | tf_op jit(solution)/shard_map/fore/pallas_call | solution.py:1241
  67.3 1.0 copy-done.9
  68.2 1.0 copy-done.10
  69.2 1.0 copy-done.11
  70.2 0.7 copy-done.17
  70.9 0.6 copy-done.20
  72.8 43.9 %attend.1 = (f32[256,2048]{1,0:T(8,128)S(1)}, f32[8,1,2048]{2,1,0:T(1,128)S(1)}, bf16[256,1024]{1,0:T(8,128)(2,1)S(1)}, bf16[1024,256]{1,0:T(8,128)(2,1)S(1)}) custom-call(s32[1]{0:T(128)S(6)} %copy.57.len_ref, bf16[768,2048]{1,0:T(8,128)(2,1)} %get-tuple-element.62.q_ref.k_ref.v_ref, bf16[768,2048]{1,0:T(8,128)(2,1)} %get-tuple-element.62.q_ref.k_ref.v_ref, ...), custom_call_target="tpu_custom_call" | custom-call | tf_op jit(solution)/shard_map/attend/pallas_call | solution.py:1273
  116.7 1.3 copy-done.1
  118.0 0.8 copy-done.12
  118.8 0.8 copy-done.13
  119.6 0.7 slice.141.out_ref
  120.3 0.6 pad.5.head_ref
  120.9 0.7 copy.51.head_bias_ref
  121.6 25.1 %middle.1 = (f32[2048,256]{1,0:T(8,128)}, bf16[256,2048]{1,0:T(8,128)(2,1)}, bf16[1152,512]{1,0:T(8,128)(2,1)}, f32[72,256]{1,0:T(8,128)}, f32[16,512]{1,0:T(8,128)}) custom-call(s32[1]{0:T(128)S(6)} %copy.57.len_ref, f32[256,2048]{1,0:T(8,128)} %copy-done.1, f32[2048,256]{1,0:T(8,128)} %get-tuple-element.65.one_ref, bf16[256,256]{1,0:T(8,128)(2,1)} %slice.141.out_ref, ...), custom_call_target="tpu_custom_call" | custom-call | tf_op jit(solution)/shard_map/middle/pallas_call | solution.py:1344
  146.7 113.0 %attend_back.1 = (bf16[256,2048]{1,0:T(8,128)(2,1)}, bf16[256,2048]{1,0:T(8,128)(2,1)}, bf16[256,2048]{1,0:T(8,128)(2,1)}, bf16[4,2,144,512]{3,2,1,0:T(8,128)(2,...) custom-call(s32[1]{0:T(128)S(6)} %copy.57.len_ref, bf16[768,2048]{1,0:T(8,128)(2,1)} %get-tuple-element.62.q_ref.k_ref.v_ref, ...), custom_call_target="tpu_custom_call" | custom-call | tf_op jit(solution)/shard_map/attend_back/pallas_call | solution.py:1312
  259.7 33.2 %hind.1 = (bf16[384,512]{1,0:T(8,128)(2,1)}, bf16[2,2304,256]{2,1,0:T(8,128)(2,1)}, f32[128,512]{1,0:T(8,128)}, f32[8,512]{1,0:T(8,128)}) custom-call(s32[1]{0:T(128)S(6)} %copy.57.len_ref, bf16[256,2048]{1,0:T(8,128)(2,1)} %get-tuple-element.71.dq_ref, bf16[256,2048]{1,0:T(8,128)(2,1)} %get-tuple-element.72.dk_ref, ...), custom_call_target="tpu_custom_call" | custom-call | tf_op jit(solution)/shard_map/hind/pallas_call | solution.py:1377
  292.9 1.7 copy-done.5
  294.5 1.0 copy-done.14
  295.5 0.9 copy-done.18
  296.5 0.7 copy-done.23
  297.2 49.7 %reduce.4 = (f32[2,288,256]{2,1,0:T(8,128)S(1)}, bf16[4,2,48,512]{3,2,1,0:T(8,128)(2,1)S(1)}, f32[4,2,16,512]{3,2,1,0:T(8,128)S(1)}, f32[3,64,512]{2,1,0:T(8,128)S(1)}, f32[8,128]{1,0:T(8,128)S(1)}) custom-call(bf16[2,4,2,288,256]{4,3,2,1,0:T(8,128)(2,1)S(1)} %bitcast.65, bf16[4,2,48,512]{3,2,1,0:T(8,128)(2,1)S(1)} %bitcast.80, ...), custom_call_target="tpu_custom_call" | custom-call | tf_op jit(solution)/shard_map/reduce/pallas_call | solution.py:1689
  347.0 0.8 fusion.13
  347.8 0.7 fusion.40
  348.6 0.9 fusion.10
  349.6 0.9 fusion.7
  351.1 0.6 multiply_reduce_fusion
  358.7 0.8 multiply_add_fusion.3
  359.5 2.2 convert.15
  361.7 3.9 slice.138
  365.6 2.3 fusion.5
  367.9 1.6 multiply_add_fusion.2
  369.6 1.8 fusion.101
  371.4 2.3 fusion.3
  373.7 1.9 fusion.6
  375.6 3.1 fusion.1
  378.7 1.5 fusion.46
  381.0 2.7 multiply_subtract_fusion
  383.7 0.6 fusion.59
  384.4 0.6 multiply_add_fusion.6
  385.0 1.2 multiply_subtract_fusion.1
  386.2 0.7 multiply_subtract_fusion.3
  386.9 0.7 multiply_subtract_fusion.2
  (104 shorter events, 4.3 us)
Async XLA Ops:
  0.7 39.8 %copy-start.44 = (f32[5896]{0:T(1024)S(1)}, f32[5896]{0:T(1024)}, u32[]{:S(2)}) copy-start(f32[5896]{0:T(1024)} %param.37) | copy-start | bytes 70756
  0.7 39.8 %copy-start.42 = (bf16[1,128,16,8]{1,3,2,0:T(8,128)(2,1)S(1)}, bf16[1,128,16,8]{1,3,2,0:T(8,128)(2,1)}, u32[]{:S(2)}) copy-start(bf16[1,128,16,8]{1,3,2,0:T(8,128)(2,1)} %param.28) | copy-start | bytes 98308
  0.7 40.3 %copy-start.43 = (bf16[1,128,16,8]{1,3,2,0:T(8,128)(2,1)S(1)}, bf16[1,128,16,8]{1,3,2,0:T(8,128)(2,1)}, u32[]{:S(2)}) copy-start(bf16[1,128,16,8]{1,3,2,0:T(8,128)(2,1)} %param.29) | copy-start | bytes 98308
  0.7 40.7 %copy-start.26 = (f32[1,512]{1,0:T(1,128)S(1)}, f32[1,512]{1,0:T(1,128)}, u32[]{:S(2)}) copy-start(f32[1,512]{1,0:T(1,128)} %clap_ref.1) | copy-start | bytes 6148
  0.7 40.7 %copy-start.16 = (f32[72,256]{1,0:T(8,128)S(1)}, f32[72,256]{1,0:T(8,128)}, u32[]{:S(2)}) copy-start(f32[72,256]{1,0:T(8,128)} %stem_ref.1) | copy-start | bytes 221188
  1.7 1.1 copy-start.3
  2.8 1.0 copy-start.7
  36.2 1.4 copy-start
  37.6 1.2 copy-start.2
  38.8 80.8 %copy-start.6 = (bf16[4,2,32,1024]{3,2,1,0:T(8,128)(2,1)}, bf16[4,2,32,1024]{3,2,1,0:T(8,128)(2,1)S(1)}, u32[]{:S(2)}) copy-start(bf16[4,2,32,1024]{3,2,1,0:T(8,128)(2,1)S(1)} %get-tuple-element.60) | copy-start | bytes 1572868
  39.6 27.7 %copy-start.22 = (f32[512]{0:T(512)}, f32[512]{0:T(512)S(1)}, u32[]{:S(2)}) copy-start(f32[512]{0:T(512)S(1)} %pad_maximum_fusion.10) | copy-start | bytes 6148
  40.5 26.7 %copy-start.15 = (f32[1,5896]{1,0:T(1,128)}, f32[1,5896]{1,0:T(1,128)S(1)}, u32[]{:S(2)}) copy-start(f32[1,5896]{1,0:T(1,128)S(1)} %broadcast_in_dim.9.vec_ref) | copy-start | bytes 70756
  41.4 31.3 %copy-start.19 = (f32[128,256]{1,0:T(8,128)S(1)}, f32[128,256]{1,0:T(8,128)}, u32[]{:S(2)}) copy-start(f32[128,256]{1,0:T(8,128)} %down_ref.2) | copy-start | bytes 393220
  67.3 1.0 copy-start.9
  68.2 1.0 copy-start.10
  69.2 1.0 copy-start.11
  70.2 0.7 copy-start.17
  70.9 0.6 copy-start.20
  71.5 0.6 copy-start.24
  72.1 0.6 copy-start.25
  72.8 47.5 %copy-start.34 = (f32[2304,8]{0,1:T(8,128)S(1)}, f32[2304,8]{0,1:T(8,128)}, u32[]{:S(2)}) copy-start(f32[2304,8]{0,1:T(8,128)} %param.35) | copy-start | bytes 221188
  116.7 1.3 copy-start.1
  118.0 0.8 copy-start.12
  118.8 0.8 copy-start.13
  119.6 0.7 copy-start.21
  292.9 1.7 copy-start.5
  294.5 1.0 copy-start.14
  295.5 0.9 copy-start.18
  296.5 0.7 copy-start.23
  297.2 50.6 %copy-start.27 = (bf16[4,2,144,512]{3,2,1,0:T(8,128)(2,1)S(1)}, bf16[4,2,144,512]{3,2,1,0:T(8,128)(2,1)}, u32[]{:S(2)}) copy-start(bf16[4,2,144,512]{3,2,1,0:T(8,128)(2,1)} %get-tuple-element.91) | copy-start | bytes 3538948
  348.5 10.2 %copy-start.31 = (f32[128,256]{1,0:T(8,128)S(1)}, f32[128,256]{1,0:T(8,128)}, u32[]{:S(2)}) copy-start(f32[128,256]{1,0:T(8,128)} %down_ref.3) | copy-start | bytes 393220
  348.6 1.0 copy-start.36
  365.6 2.3 copy-start.28
  375.6 3.1 copy-start.29
  375.6 5.4 %copy-start.4 = (f32[2,288,256]{2,1,0:T(8,128)S(1)}, f32[2,288,256]{2,1,0:T(8,128)}, u32[]{:S(2)}) copy-start(f32[2,288,256]{2,1,0:T(8,128)} %conv_ref.1) | copy-start | bytes 1769476
  375.6 5.4 %copy-start.30 = (f32[2,288,256]{2,1,0:T(8,128)S(1)}, f32[2,288,256]{2,1,0:T(8,128)}, u32[]{:S(2)}) copy-start(f32[2,288,256]{2,1,0:T(8,128)} %param.53) | copy-start | bytes 1769476
  380.2 3.5 copy-start.45
  381.0 3.4 copy-start.46
  381.0 4.0 %copy-start.8 = (f32[3,64,512]{2,1,0:T(8,128)S(1)}, f32[3,64,512]{2,1,0:T(8,128)}, u32[]{:S(2)}) copy-start(f32[3,64,512]{2,1,0:T(8,128)} %time_ref.1) | copy-start | bytes 1179652
  381.0 4.0 %copy-start.32 = (f32[3,64,512]{2,1,0:T(8,128)S(1)}, f32[3,64,512]{2,1,0:T(8,128)}, u32[]{:S(2)}) copy-start(f32[3,64,512]{2,1,0:T(8,128)} %param.49) | copy-start | bytes 1179652
  381.0 4.0 %copy-start.33 = (f32[3,64,512]{2,1,0:T(8,128)S(1)}, f32[3,64,512]{2,1,0:T(8,128)}, u32[]{:S(2)}) copy-start(f32[3,64,512]{2,1,0:T(8,128)} %param.48) | copy-start | bytes 1179652
  383.7 2.5 copy-start.38
  383.7 2.5 copy-start.39
  383.7 3.2 copy-start.35
  383.7 3.2 copy-start.40
  383.7 3.2 copy-start.41
  384.4 3.9 %copy-start.37 = (f32[5896]{0:T(1024)}, f32[5896]{0:T(1024)S(1)}, u32[]{:S(2)}) copy-start(f32[5896]{0:T(1024)S(1)} %get-tuple-element.103) | copy-start | bytes 70756
